TPU v7x, 512 devices: a whole 4x8x8 slice. The times are simulated.
512 devices in a mesh: grid: 64 (over y, z_hi, core), tm: 8 (over z_lo, x).
Axes of the slice: x: 4, y: 8, z: 8 (z_hi: 4, z_lo: 2; z = z_hi * 2 + z_lo), core: 2. Of those that a mesh axis runs over, the one named last changes fastest.
Arguments:
- observations: float32 [32, 32, 64, 768], P('tm', None, 'grid'), may hold values from -40 to 40
- a_factor: float32 [64, 256], P('grid'), may hold values from -5 to 5
- b_factor: float32 [768, 128], replicated, may hold values from -5 to 5
- c_factor: float32 [32, 16], replicated, may hold values from -5 to 5
- e_factor: float32 [32, 8], P('tm'), may hold values from -5 to 5
- core: float32 [8, 16, 128, 256], P(None, None, 'grid'), may hold values from -5 to 5
Outputs:
- residual: float32 [32, 32, 64, 768], P('tm', None, 'grid')
- a_new: float32 [64, 256], P('grid')
- b_new: float32 [768, 128], replicated
- c_new: float32 [32, 16], replicated
- e_new: float32 [32, 8], P('tm')
- core_new: float32 [8, 16, 128, 256], P(None, None, 'grid')
All inputs are finite; a program needn't handle non-finite values.
Results may differ from a plain program's by a relative error of at most 0.0003.
Values sent between devices are 32-bit elements; how exact they have to be, the bound alone decides.
No kernel may reach another device: no remote copies, remote signals or barrier semaphores. Data moves between devices by JAX's collectives and lax.ppermute only.
A program may use at most 64 MiB of HBM per device.

v0:
```python
import functools

import jax
import jax.numpy as jnp
from jax import lax
from jax.experimental import pallas as pl
from jax.experimental.pallas import tpu as pltpu
from jax.sharding import Mesh, PartitionSpec as P

STEPS = 2
ETA = 0.2
EPS = 1e-06
SCALE = float(256 * 128 * 16 * 8) ** (-0.5)

FAR = ("y", "zh")
NEAR = ("zl", "x", "co")
NF, NN = 32, 16
HIGH, FULL = lax.Precision.HIGH, lax.Precision.HIGHEST
f32 = jnp.float32


def swap(x, axes):
    return lax.all_to_all(x, axes, 0, 0, tiled=True)


def dg(a, b, ca, cb, precision=HIGH):
    return lax.dot_general(a, b, (((ca,), (cb,)), ((), ())), precision=precision, preferred_element_type=f32)


def rate(total, count):
    return ETA * lax.rsqrt(total / count + EPS)


def call(body, outs, *ins, smem=0):
    specs = [pl.BlockSpec(memory_space=pltpu.SMEM)] * smem + [pl.BlockSpec(memory_space=pltpu.VMEM)] * (len(ins) - smem)
    return pl.pallas_call(
        body,
        out_shape=[jax.ShapeDtypeStruct(s, f32) for s in outs],
        in_specs=specs,
        out_specs=[pl.BlockSpec(memory_space=pltpu.VMEM)] * len(outs),
        compiler_params=pltpu.CompilerParams(vmem_limit_bytes=32 * 1024 * 1024),
    )(*ins)


def chosen(rows, lanes, kind, start=0):
    r = lax.broadcasted_iota(jnp.int32, (rows, lanes), 0)
    n = lax.broadcasted_iota(jnp.int32, (rows, lanes), 1)
    n = n // 32 + start if kind == "h" else n % 32
    return jnp.where(r == n, 1.0, 0.0).astype(f32)


def expanded(ec_t, lanes, start=0):
    ce = dg(ec_t[:, :32], chosen(32, lanes, "v"), 1, 0, FULL)
    ee = dg(ec_t[:8, 32:64], chosen(32, lanes, "h", start), 1, 0, FULL)
    return ee, ce, (ee[:, None, :] * ce[None, :, :]).reshape(128, lanes)


def residual_body(first, *refs):
    if first:
        third_ref, c_ref, b_ref, x1_ref, gb_ref, obs_ref, ec_ref = refs
        for l in range(2):
            for t in range(8):
                obs_ref[l, :, 128 * t : 128 * t + 128] = third_ref[2 * t + l, :48, :]
        ec_t = c_ref[...]
        e_sum = third_ref[0, 64:72, :]
        for t in range(1, 8):
            e_sum = e_sum + third_ref[2 * t, 64:72, :]
        ec_t = ec_t + jnp.concatenate([e_sum, jnp.zeros_like(e_sum)], axis=0)
        ec_ref[...] = ec_t
        w = [third_ref[:, 48 + 8 * l : 56 + 8 * l, :].reshape(128, 128) for l in range(2)]
    else:
        w_ref, ec_ref, b_ref, obs_ref, x1_ref, gb_ref = refs
        ec_t = ec_ref[...]
        w = [w_ref[:, 8 * l : 8 * l + 8, :].reshape(128, 128) for l in range(2)]
    ee, ce, ec = expanded(ec_t, 1024)
    b = b_ref[...]
    bt = b.T
    gb, x = None, None
    x1_ref[:, 16:24, :] = jnp.zeros((16, 8, 128), f32)
    for l in range(2):
        q = dg(w[l].T, ec, 1, 0)
        res = SCALE * dg(b, q, 1, 0) - obs_ref[l]
        gb_l = dg(res, q, 1, 1)
        gb = gb_l if gb is None else gb + gb_l
        up = SCALE * dg(bt, res, 1, 0)
        x1_ref[:, 8 * l : 8 * l + 8, :] = dg(ec, up, 1, 1).reshape(16, 8, 128)
        x_l = dg(w[l], up, 1, 0)
        x = x_l if x is None else x + x_l
    gb_ref[...] = SCALE * gb
    x = x.reshape(8, 16, 1024)
    ge = dg(jnp.sum(x * ce[None], axis=1), chosen(32, 1024, "h"), 1, 1, FULL)
    gc = dg(jnp.sum(x * ee[:, None], axis=0), chosen(32, 1024, "v"), 1, 1, FULL)
    for r in range(16):
        x1_ref[r, 16:17, 0:32] = gc[r : r + 1]
        if r < 8:
            x1_ref[r, 16:17, 32:64] = ge[r : r + 1]


def near_sum_body(x1_ref, gb_ref, core_ref, x2_ref, ga_ref):
    s = jnp.sum(x1_ref[...], axis=0)
    acc = None
    for c in range(8):
        p = jnp.concatenate([s[c : c + 1], s[8 + c : 9 + c]], axis=0)
        t = dg(p, core_ref[c], 1, 0)
        acc = t if acc is None else acc + t
    ga_ref[...] = jnp.concatenate([acc[:, :128], acc[:, 128:], jnp.zeros((4, 128), f32)], axis=0)
    tail = jnp.concatenate([jnp.zeros((2, 128), f32), s[16:17], jnp.zeros((5, 128), f32)], axis=0)
    x2_ref[...] = jnp.broadcast_to(jnp.concatenate([s[:16], tail], axis=0)[None], (32, 24, 128))
    for k in range(24):
        x2_ref[k, 16:18, :] = gb_ref[2 * k : 2 * k + 2, :]


def core_grad_body(x2_ref, a_ref, ga_ref, x3_ref, g_ref, gb_ref):
    a = a_ref[...]
    sq = jnp.zeros((1, 128), f32)
    for c in range(8):
        p = jnp.concatenate([x2_ref[:, c, :], x2_ref[:, 8 + c, :]], axis=0)
        g = dg(p.T, a, 1, 0)
        g_ref[c] = g
        s = jnp.sum(g * g, axis=0, keepdims=True)
        sq = sq + s[:, :128] + s[:, 128:]
    s = jnp.sum(x2_ref[:, 16:24, :], axis=0)
    gb_ref[...] = s
    gb = s[0:2]
    rows = jnp.concatenate(
        [ga_ref[0:4], s[2:3], sq, jnp.sum(gb * gb, axis=0, keepdims=True), jnp.zeros((1, 128), f32)], axis=0
    )
    x3_ref[...] = jnp.broadcast_to(rows[None], (16, 8, 128))


def near_update_body(x3_ref, gb_ref, ec_ref, x4_ref, new_ref, sq_ref):
    s = jnp.sum(x3_ref[...], axis=0)
    g = x3_ref[:, 4, :]
    lane = lax.broadcasted_iota(jnp.int32, (16, 128), 1)
    gc = jnp.where(lane < 32, g, 0.0)
    ge = jnp.where(jnp.logical_and(lane >= 32, lane < 64), g, 0.0)
    new_ref[...] = ec_ref[...] - rate(jnp.sum(gc * gc), 512.0) * gc - rate(jnp.sum(ge * ge), 256.0) * ge
    sq_ref[...] = jnp.broadcast_to(jnp.sum(s[5:6], axis=1, keepdims=True), (8, 128))
    rows = jnp.concatenate([s[0:4], gb_ref[0:2], s[6:7], jnp.zeros((1, 128), f32)], axis=0)
    x4_ref[...] = jnp.broadcast_to(rows[None], (32, 8, 128))


def far_update_body(far_ref, x4_ref, a_ref, b_ref, core_ref, g_ref, sq_ref, x5_ref, a_new, b_new, core_new):
    ga = jnp.concatenate(
        [
            jnp.concatenate([x4_ref[:, 0, :], x4_ref[:, 1, :]], axis=0),
            jnp.concatenate([x4_ref[:, 2, :], x4_ref[:, 3, :]], axis=0),
        ],
        axis=1,
    )
    a_new[...] = a_ref[...] - rate(jnp.sum(ga * ga), 16384.0) * ga
    sb = jnp.sum(x4_ref[:, 6, :])
    rb = rate(sb, 98304.0)
    for k in range(24):
        b_new[2 * k : 2 * k + 2, :] = b_ref[2 * k : 2 * k + 2, :] - rb * x4_ref[k, 4:6, :]
    far = far_ref[0]
    a_two = jnp.concatenate([a_new[pl.ds(far, 1), :], a_new[pl.ds(far + 32, 1), :]], axis=0)
    rg = ETA * lax.rsqrt(sq_ref[0:1, 0:1] * (1.0 / 4194304) + EPS)
    top, low = [], []
    for c in range(8):
        g = core_ref[c] - rg * g_ref[c]
        core_new[c] = g
        w = dg(a_two, g, 1, 1)
        top.append(w[0:1])
        low.append(w[1:2])
    x5_ref[...] = jnp.broadcast_to(jnp.concatenate(top + low, axis=0)[None], (16, 16, 128))


def first_products_body(core_ref, a_ref, x_ref):
    top, low = [], []
    for c in range(8):
        w = dg(a_ref[...], core_ref[c], 1, 1)
        top.append(w[0:1])
        low.append(w[1:2])
    x_ref[...] = jnp.concatenate(top + low, axis=0)


def final_body(idx_ref, x5_ref, ec_ref, obs_ref, res_ref, b_ref):
    tm, co = idx_ref[0], idx_ref[1]
    _, _, ec = expanded(ec_ref[...], 128, 4 * tm)
    w = x5_ref[:, pl.ds(pl.multiple_of(co * 8, 8), 8), :].reshape(128, 128)
    b = x5_ref[:, 16:64, :].reshape(768, 128)
    b_ref[...] = b
    q = dg(ec.T, w, 1, 0)
    res_ref[...] = SCALE * dg(q, b, 1, 1) - obs_ref[...]


def shards(observations, a_factor, b_factor, c_factor, e_factor, core):
    tm = lax.axis_index("zl") * 4 + lax.axis_index("x")
    co = lax.axis_index("co")
    far = lax.axis_index("y") * 4 + lax.axis_index("zh")
    near = tm * 2 + co
    far_i = far.astype(jnp.int32).reshape(1)

    own = lax.dynamic_slice_in_dim(core, tm, 1, 0).reshape(2, 32, 128)
    a_own = jnp.pad(a_factor.reshape(1, 2, 128), ((0, 0), (0, 6), (0, 0)))
    first = jnp.concatenate([own, jnp.broadcast_to(a_own, (2, 8, 128))], axis=1)
    first = swap(first, "co")
    g_mine = first[:, :32].reshape(2, 8, 2, 256).transpose(1, 0, 2, 3)
    a_two = first[:, 32:34].reshape(2, 256)
    second = jnp.concatenate([g_mine.reshape(64, 128), a_two.reshape(4, 128), jnp.zeros((4, 128), f32)])
    second = swap(jnp.broadcast_to(second[None], (NF, 72, 128)), FAR)
    core_part = second[:, :64].reshape(NF, 8, 4, 256).transpose(1, 0, 2, 3).reshape(8, 128, 256)
    a_all = second[:, 64:68].reshape(NF, 2, 256).transpose(1, 0, 2).reshape(64, 256)

    obs_t = observations.reshape(128, NN, 48).transpose(1, 2, 0)
    (products,) = call(first_products_body, [(16, 128)], core_part, a_two)
    e_own = lax.dynamic_update_slice(jnp.zeros((8, 128), f32), e_factor.T, (0, 32 + 4 * tm))
    rest = jnp.concatenate([products, e_own])
    third = jnp.concatenate([obs_t, jnp.broadcast_to(rest[None], (NN, 24, 128))], axis=1)
    third = swap(third, NEAR)
    b_part = lax.dynamic_slice_in_dim(b_factor, near * 48, 48, 0)
    c_t = jnp.pad(c_factor.T, ((0, 0), (0, 96)))

    for step in range(STEPS):
        if step == 0:
            x1, gb, obs_part, ec_t = call(
                functools.partial(residual_body, True),
                [(16, 24, 128), (48, 128), (2, 48, 1024), (16, 128)],
                third, c_t, b_part,
            )
        else:
            x1, gb = call(
                functools.partial(residual_body, False), [(16, 24, 128), (48, 128)], x5, ec_t, b_part, obs_part
            )
        x2, ga = call(near_sum_body, [(32, 24, 128), (8, 128)], swap(x1, NEAR), gb, core_part)
        x3, g_core, gb = call(core_grad_body, [(16, 8, 128), (8, 128, 256), (8, 128)], swap(x2, FAR), a_all, ga)
        x4, ec_t, sq = call(near_update_body, [(32, 8, 128), (16, 128), (8, 128)], swap(x3, NEAR), gb, ec_t)
        x5, a_all, b_part, core_part = call(
            far_update_body,
            [(16, 16, 128), (64, 256), (48, 128), (8, 128, 256)],
            far_i, swap(x4, FAR), a_all, b_part, core_part, g_core, sq,
            smem=1,
        )
        if step < STEPS - 1:
            x5 = swap(x5, NEAR)

    mine = lax.dynamic_slice_in_dim(core_part, far * 4, 4, 1).reshape(8, 2, 2, 256)
    mine = mine.transpose(1, 0, 2, 3).reshape(1, 2, 32, 128)
    mine = jnp.broadcast_to(mine, (8, 2, 32, 128)).reshape(NN, 32, 128)
    x5 = swap(jnp.concatenate([x5, jnp.broadcast_to(b_part[None], (NN, 48, 128)), mine], axis=1), NEAR)
    core_new = x5[:, 64:].reshape(8, 16, 2, 256)
    idx = jnp.stack([tm, co]).astype(jnp.int32)
    residual, b_new = call(
        final_body, [(128, 768), (768, 128)], idx, x5, ec_t, observations.reshape(128, 768), smem=1
    )
    a_new = lax.dynamic_slice_in_dim(a_all, co * 32 + far, 1, 0)
    e_new = lax.dynamic_slice(ec_t, (0, 32 + 4 * tm), (8, 4)).T
    return (residual.reshape(4, 32, 1, 768), a_new, b_new, ec_t[:, :32].T, e_new, core_new)


def solution(mesh):
    fine = Mesh(mesh.devices.reshape(8, 4, 2, 2, 4), ("y", "zh", "co", "zl", "x"))
    grid, tm = ("y", "zh", "co"), ("zl", "x")
    specs = (P(tm, None, grid, None), P(grid, None), P(), P(), P(tm, None), P(None, None, grid, None))
    return jax.shard_map(shards, mesh=fine, in_specs=specs, out_specs=specs, check_vma=False)
```

profile of v0, /device:TPU:1, one launch (start us, length us, event | category | flops | bytes accessed | tf_op | source)
XLA Modules:
  0.0 246.7 jit_solution(17978120086866060825)
XLA Ops:
  2.2 10.3 %all_to_all.65 = f32[2,40,128]{2,1,0:T(8,128)S(1)} all-to-all(f32[2,40,128]{2,1,0:T(8,128)S(1)} %pad_maximum_fusion.2), channel_id=1, replica_groups=mesh['y'=8,'zh'=4,'co'=2,'zl'=2,'x'=4] {'co'}, dimensions={0} | all-to-all | bytes 81920 | tf_op jit(solution)/shard_map/all_to_all | solution.py:23
  12.7 1.1 broadcast_in_dim.41
  13.9 10.4 %all-to-all-start.1 = ((f32[32,72,128]{2,1,0:T(8,128)}), f32[32,72,128]{2,1,0:T(8,128)S(1)}, u32[]{:S(2)}, u32[]{:S(2)}) async-start(f32[32,72,128]{2,1,0:T(8,128)} %broadcast_in_dim.41), calls=%async_computation.1 | async-start | bytes 2359296 | tf_op jit(solution)/shard_map/all_to_all | solution.py:23
  24.4 1.8 reduce
  26.2 1.5 reshape.66
  28.5 27.4 %all-to-all-done.1 = f32[32,72,128]{2,1,0:T(8,128)S(1)} async-done(((f32[32,72,128]{2,1,0:T(8,128)}), f32[32,72,128]{2,1,0:T(8,128)S(1)}, u32[]{:S(2)}, u32[]{:S(2)}) %all-to-all-start.1) | async-done | bytes 1179680 | tf_op jit(solution)/shard_map/all_to_all | solution.py:23
  55.9 1.1 slice.26
  57.0 1.7 reshape.71
  58.7 1.2 copy.25
  59.8 1.6 reshape.72.core_ref
  62.9 6.7 %all-to-all-start.2 = ((f32[16,72,128]{2,1,0:T(8,128)}), f32[16,72,128]{2,1,0:T(8,128)S(1)}, u32[]{:S(2)}, u32[]{:S(2)}) async-start(f32[16,72,128]{2,1,0:T(8,128)} %pad_maximum_fusion.1), calls=%async_computation.2 | async-start | bytes 1179648 | tf_op jit(solution)/shard_map/all_to_all | solution.py:23
  69.6 10.5 %all-to-all-done.2.refs_0_ = f32[16,72,128]{2,1,0:T(8,128)S(1)} async-done(((f32[16,72,128]{2,1,0:T(8,128)}), f32[16,72,128]{2,1,0:T(8,128)S(1)}, u32[]{:S(2)}, u32[]{:S(2)}) %all-to-all-start.2) | async-done | bytes 589856 | tf_op jit(solution)/shard_map/all_to_all | solution.py:23
  80.0 3.7 %shard_map.110 = (f32[16,24,128]{2,1,0:T(8,128)S(1)}, f32[48,128]{1,0:T(8,128)S(1)}, f32[2,48,1024]{2,1,0:T(8,128)S(1)}, f32[16,128]{1,0:T(8,128)S(1)}) custom-call(f32[16,72,128]{2,1,0:T(8,128)S(1)} %all-to-all-done.2.refs_0_, f32[16,128]{1,0:T(8,128)S(1)} %pad.9.refs_1_, f32[48,128]{1,0:T(8,128)S(1)} %constant_dynamic-slice_fusion.2.refs_2_.b_ref), custom_call_target="tpu_custom_call" | custom-call | tf_op jit(solution)/shard_map/pallas_call | solution.py:36
  84.5 10.3 %all_to_all.66.x1_ref = f32[16,24,128]{2,1,0:T(8,128)S(1)} all-to-all(f32[16,24,128]{2,1,0:T(8,128)S(1)} %get-tuple-element.38), channel_id=1, replica_groups=mesh['y'=8,'zh'=4,'co'=2,'zl'=2,'x'=4] {'zl','x','co'}, dimensions={0} | all-to-all | bytes 393216 | tf_op jit(solution)/shard_map/all_to_all | solution.py:23
  94.8 1.0 shard_map.111
  95.8 7.2 %all-to-all-start.4 = ((f32[32,24,128]{2,1,0:T(8,128)}), f32[32,24,128]{2,1,0:T(8,128)S(1)}, u32[]{:S(2)}, u32[]{:S(2)}) async-start(f32[32,24,128]{2,1,0:T(8,128)} %get-tuple-element.40), calls=%async_computation.4 | async-start | bytes 786432 | tf_op jit(solution)/shard_map/all_to_all | solution.py:23
  103.1 14.5 %all-to-all-done.4.x2_ref = f32[32,24,128]{2,1,0:T(8,128)S(1)} async-done(((f32[32,24,128]{2,1,0:T(8,128)}), f32[32,24,128]{2,1,0:T(8,128)S(1)}, u32[]{:S(2)}, u32[]{:S(2)}) %all-to-all-start.4) | async-done | bytes 393248 | tf_op jit(solution)/shard_map/all_to_all | solution.py:23
  118.3 11.0 %all_to_all.67.x3_ref = f32[16,8,128]{2,1,0:T(8,128)S(1)} all-to-all(f32[16,8,128]{2,1,0:T(8,128)S(1)} %get-tuple-element.42), channel_id=1, replica_groups=mesh['y'=8,'zh'=4,'co'=2,'zl'=2,'x'=4] {'zl','x','co'}, dimensions={0} | all-to-all | bytes 131072 | tf_op jit(solution)/shard_map/all_to_all | solution.py:23
  130.0 5.0 %all-to-all-start.6 = ((f32[32,8,128]{2,1,0:T(8,128)}), f32[32,8,128]{2,1,0:T(8,128)S(1)}, u32[]{:S(2)}, u32[]{:S(2)}) async-start(f32[32,8,128]{2,1,0:T(8,128)} %get-tuple-element.45), calls=%async_computation.6 | async-start | bytes 262144 | tf_op jit(solution)/shard_map/all_to_all | solution.py:23
  135.1 11.3 %all-to-all-done.6.x4_ref = f32[32,8,128]{2,1,0:T(8,128)S(1)} async-done(((f32[32,8,128]{2,1,0:T(8,128)}), f32[32,8,128]{2,1,0:T(8,128)S(1)}, u32[]{:S(2)}, u32[]{:S(2)}) %all-to-all-start.6) | async-done | bytes 131104 | tf_op jit(solution)/shard_map/all_to_all | solution.py:23
  150.4 10.6 %all_to_all.68.refs_0_ = f32[16,16,128]{2,1,0:T(8,128)S(1)} all-to-all(f32[16,16,128]{2,1,0:T(8,128)S(1)} %get-tuple-element.48), channel_id=1, replica_groups=mesh['y'=8,'zh'=4,'co'=2,'zl'=2,'x'=4] {'zl','x','co'}, dimensions={0} | all-to-all | bytes 262144 | tf_op jit(solution)/shard_map/all_to_all | solution.py:23
  161.0 3.7 %shard_map.115 = (f32[16,24,128]{2,1,0:T(8,128)S(1)}, f32[48,128]{1,0:T(8,128)S(1)}) custom-call(f32[16,16,128]{2,1,0:T(8,128)S(1)} %all_to_all.68.refs_0_, f32[16,128]{1,0:T(8,128)S(1)} %get-tuple-element.49.refs_1_.ec_ref, f32[48,128]{1,0:T(8,128)S(1)} %get-tuple-element.50.refs_2_.b_ref, f32[2,48,1024]{2,1,0:T(8,128)S(1)} %copy-done.6), custom_call_target="tpu_custom_call" | custom-call | tf_op jit(solution)/shard_map/pallas_call | solution.py:36
  164.7 9.8 %all_to_all.69.x1_ref = f32[16,24,128]{2,1,0:T(8,128)S(1)} all-to-all(f32[16,24,128]{2,1,0:T(8,128)S(1)} %get-tuple-element.52), channel_id=1, replica_groups=mesh['y'=8,'zh'=4,'co'=2,'zl'=2,'x'=4] {'zl','x','co'}, dimensions={0} | all-to-all | bytes 393216 | tf_op jit(solution)/shard_map/all_to_all | solution.py:23
  174.9 17.8 %all_to_all.70.x2_ref = f32[32,24,128]{2,1,0:T(8,128)S(1)} all-to-all(f32[32,24,128]{2,1,0:T(8,128)S(1)} %get-tuple-element.55), channel_id=1, replica_groups=mesh['y'=8,'zh'=4,'co'=2,'zl'=2,'x'=4] {'y','zh'}, dimensions={0} | all-to-all | bytes 786432 | tf_op jit(solution)/shard_map/all_to_all | solution.py:23
  193.4 11.0 %all_to_all.71.x3_ref = f32[16,8,128]{2,1,0:T(8,128)S(1)} all-to-all(f32[16,8,128]{2,1,0:T(8,128)S(1)} %get-tuple-element.58), channel_id=1, replica_groups=mesh['y'=8,'zh'=4,'co'=2,'zl'=2,'x'=4] {'zl','x','co'}, dimensions={0} | all-to-all | bytes 131072 | tf_op jit(solution)/shard_map/all_to_all | solution.py:23
  205.1 5.0 %all-to-all-start.11 = ((f32[32,8,128]{2,1,0:T(8,128)}), f32[32,8,128]{2,1,0:T(8,128)S(1)}, u32[]{:S(2)}, u32[]{:S(2)}) async-start(f32[32,8,128]{2,1,0:T(8,128)} %get-tuple-element.60), calls=%async_computation.11 | async-start | bytes 262144 | tf_op jit(solution)/shard_map/all_to_all | solution.py:23
  210.1 11.3 %all-to-all-done.11.x4_ref = f32[32,8,128]{2,1,0:T(8,128)S(1)} async-done(((f32[32,8,128]{2,1,0:T(8,128)}), f32[32,8,128]{2,1,0:T(8,128)S(1)}, u32[]{:S(2)}, u32[]{:S(2)}) %all-to-all-start.11) | async-done | bytes 131104 | tf_op jit(solution)/shard_map/all_to_all | solution.py:23
  223.3 1.0 pad_maximum_fusion
  224.3 5.5 %all-to-all-start.12 = ((f32[16,96,128]{2,1,0:T(8,128)}), f32[16,96,128]{2,1,0:T(8,128)S(1)}, u32[]{:S(2)}, u32[]{:S(2)}) async-start(f32[16,96,128]{2,1,0:T(8,128)} %pad_maximum_fusion), calls=%async_computation.12 | async-start | bytes 1572864 | tf_op jit(solution)/shard_map/all_to_all | solution.py:23
  231.8 11.0 %all-to-all-done.12.x5_ref = f32[16,96,128]{2,1,0:T(8,128)S(1)} async-done(((f32[16,96,128]{2,1,0:T(8,128)}), f32[16,96,128]{2,1,0:T(8,128)S(1)}, u32[]{:S(2)}, u32[]{:S(2)}) %all-to-all-start.12) | async-done | bytes 786464 | tf_op jit(solution)/shard_map/all_to_all | solution.py:23
  242.8 1.8 shard_map.120
  244.6 1.1 copy.30
  (82 shorter events, 16.6 us)
Async XLA Ops:
  0.6 68.9 %copy-start = (f32[768,128]{1,0:T(8,128)S(1)}, f32[768,128]{1,0:T(8,128)}, u32[]{:S(2)}) copy-start(f32[768,128]{1,0:T(8,128)} %param.8) | copy-start | bytes 1179652
  13.9 10.5 %copy-start.16 = (f32[4,8]{1,0:T(4,128)S(1)}, f32[4,8]{1,0:T(4,128)}, u32[]{:S(2)}) copy-start(f32[4,8]{1,0:T(4,128)} %param.10) | copy-start | bytes 388
  13.9 10.6 %copy-start.13 = (f32[4,32,1,768]{3,2,1,0:T(1,128)S(1)}, f32[4,32,1,768]{3,2,1,0:T(1,128)}, u32[]{:S(2)}) copy-start(f32[4,32,1,768]{3,2,1,0:T(1,128)} %param.6) | copy-start | bytes 1179652
  13.9 42.0 %all-to-all-start.1 = ((f32[32,72,128]{2,1,0:T(8,128)}), f32[32,72,128]{2,1,0:T(8,128)S(1)}, u32[]{:S(2)}, u32[]{:S(2)}) async-start(f32[32,72,128]{2,1,0:T(8,128)} %broadcast_in_dim.41), calls=%async_computation.1 | async-start | bytes 2359296 | tf_op jit(solution)/shard_map/all_to_all | solution.py:23
  62.0 7.5 %copy-start.15 = (f32[32,16]{0,1:T(8,128)S(1)}, f32[32,16]{0,1:T(8,128)}, u32[]{:S(2)}) copy-start(f32[32,16]{0,1:T(8,128)} %param.9) | copy-start | bytes 6148
  62.9 17.2 %all-to-all-start.2 = ((f32[16,72,128]{2,1,0:T(8,128)}), f32[16,72,128]{2,1,0:T(8,128)S(1)}, u32[]{:S(2)}, u32[]{:S(2)}) async-start(f32[16,72,128]{2,1,0:T(8,128)} %pad_maximum_fusion.1), calls=%async_computation.2 | async-start | bytes 1179648 | tf_op jit(solution)/shard_map/all_to_all | solution.py:23
  69.6 26.3 %copy-start.9 = (f32[48,128]{1,0:T(8,128)}, f32[48,128]{1,0:T(8,128)S(1)}, u32[]{:S(2)}) copy-start(f32[48,128]{1,0:T(8,128)S(1)} %constant_dynamic-slice_fusion.2.refs_2_.b_ref) | copy-start | bytes 73732
  83.7 0.8 copy-start.5
  95.8 21.8 %all-to-all-start.4 = ((f32[32,24,128]{2,1,0:T(8,128)}), f32[32,24,128]{2,1,0:T(8,128)S(1)}, u32[]{:S(2)}, u32[]{:S(2)}) async-start(f32[32,24,128]{2,1,0:T(8,128)} %get-tuple-element.40), calls=%async_computation.4 | async-start | bytes 786432 | tf_op jit(solution)/shard_map/all_to_all | solution.py:23
  103.1 43.9 %copy-start.1 = (f32[2,32,256]{2,1,0:T(8,128)}, f32[2,32,256]{2,1,0:T(8,128)S(1)}, u32[]{:S(2)}) copy-start(f32[2,32,256]{2,1,0:T(8,128)S(1)} %copy.27) | copy-start | bytes 196612
  130.0 16.3 %all-to-all-start.6 = ((f32[32,8,128]{2,1,0:T(8,128)}), f32[32,8,128]{2,1,0:T(8,128)S(1)}, u32[]{:S(2)}, u32[]{:S(2)}) async-start(f32[32,8,128]{2,1,0:T(8,128)} %get-tuple-element.45), calls=%async_computation.6 | async-start | bytes 262144 | tf_op jit(solution)/shard_map/all_to_all | solution.py:23
  146.4 0.7 copy-start.3
  147.0 0.8 copy-start.2
  147.9 0.9 copy-start.4
  148.8 0.7 copy-start.10
  149.5 11.5 %copy-start.6 = (f32[2,48,1024]{2,1,0:T(8,128)S(1)}, f32[2,48,1024]{2,1,0:T(8,128)}, u32[]{:S(2)}) copy-start(f32[2,48,1024]{2,1,0:T(8,128)} %copy-done.5) | copy-start | bytes 1179652
  150.4 24.5 %copy-start.11 = (f32[48,128]{1,0:T(8,128)}, f32[48,128]{1,0:T(8,128)S(1)}, u32[]{:S(2)}) copy-start(f32[48,128]{1,0:T(8,128)S(1)} %get-tuple-element.50.refs_2_.b_ref) | copy-start | bytes 73732
  150.4 42.3 %copy-start.7 = (f32[64,256]{1,0:T(8,128)}, f32[64,256]{1,0:T(8,128)S(1)}, u32[]{:S(2)}) copy-start(f32[64,256]{1,0:T(8,128)S(1)} %get-tuple-element.56.a_ref) | copy-start | bytes 196612
  174.9 46.5 %copy-start.12 = (f32[48,128]{1,0:T(8,128)S(1)}, f32[48,128]{1,0:T(8,128)}, u32[]{:S(2)}) copy-start(f32[48,128]{1,0:T(8,128)} %copy-done.11) | copy-start | bytes 73732
  205.1 16.3 %all-to-all-start.11 = ((f32[32,8,128]{2,1,0:T(8,128)}), f32[32,8,128]{2,1,0:T(8,128)S(1)}, u32[]{:S(2)}, u32[]{:S(2)}) async-start(f32[32,8,128]{2,1,0:T(8,128)} %get-tuple-element.60), calls=%async_computation.11 | async-start | bytes 262144 | tf_op jit(solution)/shard_map/all_to_all | solution.py:23
  221.4 0.8 copy-start.8
  224.2 5.5 %copy-start.14 = (f32[4,32,1,768]{3,2,1,0:T(1,128)S(1)}, f32[4,32,1,768]{3,2,1,0:T(1,128)}, u32[]{:S(2)}) copy-start(f32[4,32,1,768]{3,2,1,0:T(1,128)} %param.6) | copy-start | bytes 1179652
  224.3 18.6 %all-to-all-start.12 = ((f32[16,96,128]{2,1,0:T(8,128)}), f32[16,96,128]{2,1,0:T(8,128)S(1)}, u32[]{:S(2)}, u32[]{:S(2)}) async-start(f32[16,96,128]{2,1,0:T(8,128)} %pad_maximum_fusion), calls=%async_computation.12 | async-start | bytes 1572864 | tf_op jit(solution)/shard_map/all_to_all | solution.py:23
where the time goes:
time: 248 us; the launch traced here: 247 us
  waiting for transfers between devices  86.1 us (35%)
  blocking collectives  80.9 us (33%)
  starting transfers between devices  39.8 us (16%)
  local copies, waits for them, and re-layouts  19.7 us (8%)
  Pallas kernels  15.4 us (6%)
  other arithmetic  3.75 us (2%)
    all_to_all x6, waiting for transfers between devices, swap(): return lax.all_to_all(x, axes, 0, 0, tiled=True)  86.1 us
    all_to_all x7, blocking collectives, swap(): return lax.all_to_all(x, axes, 0, 0, tiled=True)  80.9 us
    all_to_all x6, starting transfers between devices, swap(): return lax.all_to_all(x, axes, 0, 0, tiled=True)  39.8 us
    pallas_call x12, Pallas kernels, call(): pl.pallas_call(body, out_shape=[jax.ShapeDtypeStruct(s, f32) for s in out...  15.4 us
    unnamed x40, local copies, waits for them, and re-layouts  6.71 us
  transfers between devices with their start and end apart: 6, of which 6 were waited for; matrix products, arithmetic and copies ran while one was open for 3% of the time, Pallas kernels for 0%

commit v1 on v0

--- a/solution.py
+++ b/solution.py
@@ -31,14 +31,14 @@
     return ETA * lax.rsqrt(total / count + EPS)
 
 
-def call(body, outs, *ins, smem=0):
+def call(body, outs, *ins, smem=0, mib=10):
     specs = [pl.BlockSpec(memory_space=pltpu.SMEM)] * smem + [pl.BlockSpec(memory_space=pltpu.VMEM)] * (len(ins) - smem)
     return pl.pallas_call(
         body,
         out_shape=[jax.ShapeDtypeStruct(s, f32) for s in outs],
         in_specs=specs,
         out_specs=[pl.BlockSpec(memory_space=pltpu.VMEM)] * len(outs),
-        compiler_params=pltpu.CompilerParams(vmem_limit_bytes=32 * 1024 * 1024),
+        compiler_params=pltpu.CompilerParams(vmem_limit_bytes=mib * 1024 * 1024),
     )(*ins)
 
 
@@ -96,6 +96,16 @@
             x1_ref[r, 16:17, 32:64] = ge[r : r + 1]
 
 
+def products(a_ref, far, core):
+    a_two = jnp.concatenate([a_ref[pl.ds(far, 1), :], a_ref[pl.ds(far + 32, 1), :]], axis=0)
+    top, low = [], []
+    for g in core:
+        w = dg(a_two, g, 1, 1)
+        top.append(w[0:1])
+        low.append(w[1:2])
+    return jnp.concatenate(top + low, axis=0)
+
+
 def near_sum_body(x1_ref, gb_ref, core_ref, x2_ref, ga_ref):
     s = jnp.sum(x1_ref[...], axis=0)
     acc = None
@@ -140,7 +150,7 @@
     x4_ref[...] = jnp.broadcast_to(rows[None], (32, 8, 128))
 
 
-def far_update_body(far_ref, x4_ref, a_ref, b_ref, core_ref, g_ref, sq_ref, x5_ref, a_new, b_new, core_new):
+def far_update_body(last, far_ref, x4_ref, a_ref, b_ref, core_ref, g_ref, sq_ref, x5_ref, a_new, *rest):
     ga = jnp.concatenate(
         [
             jnp.concatenate([x4_ref[:, 0, :], x4_ref[:, 1, :]], axis=0),
@@ -149,40 +159,78 @@
         axis=1,
     )
     a_new[...] = a_ref[...] - rate(jnp.sum(ga * ga), 16384.0) * ga
-    sb = jnp.sum(x4_ref[:, 6, :])
-    rb = rate(sb, 98304.0)
-    for k in range(24):
-        b_new[2 * k : 2 * k + 2, :] = b_ref[2 * k : 2 * k + 2, :] - rb * x4_ref[k, 4:6, :]
+    rb = rate(jnp.sum(x4_ref[:, 6, :]), 98304.0)
+    gb = jnp.concatenate([x4_ref[k, 4:6, :] for k in range(24)], axis=0)
+    b_new = b_ref[...] - rb * gb
     far = far_ref[0]
-    a_two = jnp.concatenate([a_new[pl.ds(far, 1), :], a_new[pl.ds(far + 32, 1), :]], axis=0)
     rg = ETA * lax.rsqrt(sq_ref[0:1, 0:1] * (1.0 / 4194304) + EPS)
-    top, low = [], []
+    core = [core_ref[c] - rg * g_ref[c] for c in range(8)]
+    x5_ref[:, 0:16, :] = jnp.broadcast_to(products(a_new, far, core)[None], (16, 16, 128))
+    if not last:
+        b_out, core_out = rest
+        b_out[...] = b_new
+        for c in range(8):
+            core_out[c] = core[c]
+        return
+    x5_ref[:, 16:64, :] = jnp.broadcast_to(b_new[None], (16, 48, 128))
+    at = pl.ds(pl.multiple_of(far // 2 * 8, 8), 8)
+    own = [[], []]
     for c in range(8):
-        g = core_ref[c] - rg * g_ref[c]
-        core_new[c] = g
-        w = dg(a_two, g, 1, 1)
-        top.append(w[0:1])
-        low.append(w[1:2])
-    x5_ref[...] = jnp.broadcast_to(jnp.concatenate(top + low, axis=0)[None], (16, 16, 128))
-
-
-def first_products_body(core_ref, a_ref, x_ref):
-    top, low = [], []
-    for c in range(8):
-        w = dg(a_ref[...], core_ref[c], 1, 1)
-        top.append(w[0:1])
-        low.append(w[1:2])
-    x_ref[...] = jnp.concatenate(top + low, axis=0)
-
-
-def final_body(idx_ref, x5_ref, ec_ref, obs_ref, res_ref, b_ref):
+        v = core_ref[c, at, :] - rg * g_ref[c, at, :]
+        v = jnp.where(far % 2 == 0, v[0:4], v[4:8])
+        for co in range(2):
+            own[co] += [v[2 * co : 2 * co + 2, :128], v[2 * co : 2 * co + 2, 128:]]
+    for co in range(2):
+        rows = jnp.concatenate(own[co], axis=0)
+        for t in range(8):
+            x5_ref[2 * t + co, 64:96, :] = rows
+
+
+def pack_body(tm_ref, core_ref, a_ref, out_ref):
+    rows = core_ref[tm_ref[0]]
+    for k in range(2):
+        out_ref[k, 0:32, :] = rows[32 * k : 32 * k + 32]
+        out_ref[k, 32:34, :] = a_ref[...]
+        out_ref[k, 34:40, :] = jnp.zeros((6, 128), f32)
+
+
+def spread_body(first_ref, out_ref):
+    parts = []
+    for k in range(16):
+        parts += [first_ref[co, 2 * k : 2 * k + 2, :] for co in range(2)]
+    for half in range(2):
+        parts += [first_ref[l, 32 + half : 33 + half, :] for l in range(2)]
+    parts.append(jnp.zeros((4, 128), f32))
+    rows = jnp.concatenate(parts, axis=0)
+    out_ref[...] = jnp.broadcast_to(rows[None], (32, 72, 128))
+
+
+def first_products_body(far_ref, second_ref, obs_ref, e_ref, third_ref, core_ref, a_ref):
+    for k in range(32):
+        for c in range(8):
+            for half in range(2):
+                r = 4 * (2 * c + half)
+                core_ref[c, 4 * k : 4 * k + 4, 128 * half : 128 * half + 128] = second_ref[k, r : r + 4, :]
+    for half in range(2):
+        for l in range(2):
+            a_ref[32 * l : 32 * l + 32, 128 * half : 128 * half + 128] = second_ref[:, 64 + 2 * half + l, :]
+    x = jnp.concatenate([products(a_ref, far_ref[0], [core_ref[c] for c in range(8)]), e_ref[...]], axis=0)
+    third_ref[:, 48:72, :] = jnp.broadcast_to(x[None], (16, 24, 128))
+    obs_t = jnp.concatenate([obs_ref[pl.ds(j, 128, stride=6), :].T for j in range(6)], axis=0)
+    third_ref[:, 0:48, :] = obs_t.reshape(16, 48, 128)
+
+
+def final_body(idx_ref, x5_ref, ec_ref, obs_ref, res_ref, b_ref, core_ref):
     tm, co = idx_ref[0], idx_ref[1]
     _, _, ec = expanded(ec_ref[...], 128, 4 * tm)
     w = x5_ref[:, pl.ds(pl.multiple_of(co * 8, 8), 8), :].reshape(128, 128)
     b = x5_ref[:, 16:64, :].reshape(768, 128)
     b_ref[...] = b
+    core_ref[...] = x5_ref[:, 64:96, :].reshape(512, 128)
     q = dg(ec.T, w, 1, 0)
-    res_ref[...] = SCALE * dg(q, b, 1, 1) - obs_ref[...]
+    for j in range(6):
+        at = pl.ds(j, 128, stride=6)
+        res_ref[at, :] = SCALE * dg(q, b[128 * j : 128 * j + 128], 1, 1) - obs_ref[at, :]
 
 
 def shards(observations, a_factor, b_factor, c_factor, e_factor, core):
@@ -192,22 +240,14 @@
     near = tm * 2 + co
     far_i = far.astype(jnp.int32).reshape(1)
 
-    own = lax.dynamic_slice_in_dim(core, tm, 1, 0).reshape(2, 32, 128)
-    a_own = jnp.pad(a_factor.reshape(1, 2, 128), ((0, 0), (0, 6), (0, 0)))
-    first = jnp.concatenate([own, jnp.broadcast_to(a_own, (2, 8, 128))], axis=1)
-    first = swap(first, "co")
-    g_mine = first[:, :32].reshape(2, 8, 2, 256).transpose(1, 0, 2, 3)
-    a_two = first[:, 32:34].reshape(2, 256)
-    second = jnp.concatenate([g_mine.reshape(64, 128), a_two.reshape(4, 128), jnp.zeros((4, 128), f32)])
-    second = swap(jnp.broadcast_to(second[None], (NF, 72, 128)), FAR)
-    core_part = second[:, :64].reshape(NF, 8, 4, 256).transpose(1, 0, 2, 3).reshape(8, 128, 256)
-    a_all = second[:, 64:68].reshape(NF, 2, 256).transpose(1, 0, 2).reshape(64, 256)
-
-    obs_t = observations.reshape(128, NN, 48).transpose(1, 2, 0)
-    (products,) = call(first_products_body, [(16, 128)], core_part, a_two)
+    rows = core.reshape(8, 16, 2, 2, 128).transpose(0, 1, 3, 2, 4).reshape(8, 64, 128)
+    (first,) = call(pack_body, [(2, 40, 128)], tm.astype(jnp.int32).reshape(1), rows, a_factor.reshape(2, 128), smem=1)
+    (second,) = call(spread_body, [(32, 72, 128)], swap(first, "co"))
+    obs = observations.reshape(768, 128)
     e_own = lax.dynamic_update_slice(jnp.zeros((8, 128), f32), e_factor.T, (0, 32 + 4 * tm))
-    rest = jnp.concatenate([products, e_own])
-    third = jnp.concatenate([obs_t, jnp.broadcast_to(rest[None], (NN, 24, 128))], axis=1)
+    third, core_part, a_all = call(
+        first_products_body, [(16, 72, 128), (8, 128, 256), (64, 256)], far_i, swap(second, FAR), obs, e_own, smem=1
+    )
     third = swap(third, NEAR)
     b_part = lax.dynamic_slice_in_dim(b_factor, near * 48, 48, 0)
     c_t = jnp.pad(c_factor.T, ((0, 0), (0, 96)))
@@ -217,33 +257,32 @@
             x1, gb, obs_part, ec_t = call(
                 functools.partial(residual_body, True),
                 [(16, 24, 128), (48, 128), (2, 48, 1024), (16, 128)],
-                third, c_t, b_part,
+                third, c_t, b_part, mib=16,
             )
         else:
             x1, gb = call(
-                functools.partial(residual_body, False), [(16, 24, 128), (48, 128)], x5, ec_t, b_part, obs_part
+                functools.partial(residual_body, False), [(16, 24, 128), (48, 128)], x5, ec_t, b_part, obs_part, mib=16
             )
         x2, ga = call(near_sum_body, [(32, 24, 128), (8, 128)], swap(x1, NEAR), gb, core_part)
         x3, g_core, gb = call(core_grad_body, [(16, 8, 128), (8, 128, 256), (8, 128)], swap(x2, FAR), a_all, ga)
         x4, ec_t, sq = call(near_update_body, [(32, 8, 128), (16, 128), (8, 128)], swap(x3, NEAR), gb, ec_t)
-        x5, a_all, b_part, core_part = call(
-            far_update_body,
-            [(16, 16, 128), (64, 256), (48, 128), (8, 128, 256)],
+        last = step == STEPS - 1
+        more = [] if last else [(48, 128), (8, 128, 256)]
+        x5, a_all, *rest = call(
+            functools.partial(far_update_body, last),
+            [(16, 96 if last else 16, 128), (64, 256)] + more,
             far_i, swap(x4, FAR), a_all, b_part, core_part, g_core, sq,
             smem=1,
         )
-        if step < STEPS - 1:
-            x5 = swap(x5, NEAR)
-
-    mine = lax.dynamic_slice_in_dim(core_part, far * 4, 4, 1).reshape(8, 2, 2, 256)
-    mine = mine.transpose(1, 0, 2, 3).reshape(1, 2, 32, 128)
-    mine = jnp.broadcast_to(mine, (8, 2, 32, 128)).reshape(NN, 32, 128)
-    x5 = swap(jnp.concatenate([x5, jnp.broadcast_to(b_part[None], (NN, 48, 128)), mine], axis=1), NEAR)
-    core_new = x5[:, 64:].reshape(8, 16, 2, 256)
+        x5 = swap(x5, NEAR)
+        if not last:
+            b_part, core_part = rest
+
     idx = jnp.stack([tm, co]).astype(jnp.int32)
-    residual, b_new = call(
-        final_body, [(128, 768), (768, 128)], idx, x5, ec_t, observations.reshape(128, 768), smem=1
-    )
+    residual, b_new, core_new = call(
+        final_body, [(768, 128), (768, 128), (512, 128)], idx, x5, ec_t, obs, smem=1
+    )
+    core_new = core_new.reshape(8, 16, 2, 2, 128).transpose(0, 1, 3, 2, 4).reshape(8, 16, 2, 256)
     a_new = lax.dynamic_slice_in_dim(a_all, co * 32 + far, 1, 0)
     e_new = lax.dynamic_slice(ec_t, (0, 32 + 4 * tm), (8, 4)).T
     return (residual.reshape(4, 32, 1, 768), a_new, b_new, ec_t[:, :32].T, e_new, core_new)

time: 248 us -> 233 us (0.940)
  blocking collectives: 80.9 us -> 135 us
  waiting for transfers between devices: 86.1 us -> 52.9 us
  starting transfers between devices: 39.8 us -> 22.5 us
  local copies, waits for them, and re-layouts: 19.7 us -> 4.73 us
  other arithmetic: 3.75 us -> 0.07 us
    all_to_all x7 -> x10, blocking collectives: 80.9 us -> 135 us  [swap(): return lax.all_to_all(x, axes, 0, 0, tiled=True)]
    all_to_all x6 -> x3, waiting for transfers between devices: 86.1 us -> 52.9 us  [swap(): return lax.all_to_all(x, axes, 0, 0, tiled=True)]
    all_to_all x6 -> x3, starting transfers between devices: 39.8 us -> 22.5 us  [swap(): return lax.all_to_all(x, axes, 0, 0, tiled=True)]
    reshape x9 -> x0, local copies, waits for them, and re-layouts: 6.25 us -> none  [the longest x2 3.28 us: shards(): second[:, :64].reshape(NF, 8, 4, 256).transpose(1, 0, 2, 3)]
    unnamed x40 -> x16, local copies, waits for them, and re-layouts: 6.71 us -> 3.25 us
    pallas_call x12 -> x14, Pallas kernels: 15.4 us -> 16.4 us  [call(): pl.pallas_call(body, out_shape=[jax.ShapeDtypeStruct(s, f32) for s in out...]
  transfers between devices with their start and end apart: 6 -> 3, of which waited for: 6 -> 3; matrix products, arithmetic and copies ran while one was open for 3% -> 1% of each run, Pallas kernels for 0% -> 0%
where the time goes in v1:
time: 233 us; the launch traced here: 232 us
  blocking collectives  135 us (58%)
  waiting for transfers between devices  52.9 us (23%)
  starting transfers between devices  22.5 us (10%)
  Pallas kernels  16.4 us (7%)
  local copies, waits for them, and re-layouts  4.73 us (2%)
    all_to_all x10, blocking collectives, swap(): return lax.all_to_all(x, axes, 0, 0, tiled=True)  135 us
    all_to_all x3, waiting for transfers between devices, swap(): return lax.all_to_all(x, axes, 0, 0, tiled=True)  52.9 us
    all_to_all x3, starting transfers between devices, swap(): return lax.all_to_all(x, axes, 0, 0, tiled=True)  22.5 us
    pallas_call x14, Pallas kernels, call(): pl.pallas_call(body, out_shape=[jax.ShapeDtypeStruct(s, f32) for s in out...  16.4 us
  transfers between devices with their start and end apart: 3, of which 3 were waited for; matrix products, arithmetic and copies ran while one was open for 1% of the time, Pallas kernels for 0%

profile of v1, /device:TPU:1, one launch (start us, length us, event | category | flops | bytes accessed | tf_op | source)
XLA Modules:
  0.0 231.9 jit_solution(4903772861014315597)
XLA Ops:
  0.7 1.0 copy-done.3
  1.7 0.7 copy-done.4
  2.3 10.3 %all_to_all.65.first_ref = f32[2,40,128]{2,1,0:T(8,128)S(1)} all-to-all(f32[2,40,128]{2,1,0:T(8,128)S(1)} %shard_map.109), channel_id=1, replica_groups=mesh['y'=8,'zh'=4,'co'=2,'zl'=2,'x'=4] {'co'}, dimensions={0} | all-to-all | bytes 81920 | tf_op jit(solution)/shard_map/all_to_all | solution.py:23
  12.6 1.1 shard_map.110
  13.7 10.4 %all-to-all-start.1 = ((f32[32,72,128]{2,1,0:T(8,128)}), f32[32,72,128]{2,1,0:T(8,128)S(1)}, u32[]{:S(2)}, u32[]{:S(2)}) async-start(f32[32,72,128]{2,1,0:T(8,128)} %shard_map.110), calls=%async_computation.1 | async-start | bytes 2359296 | tf_op jit(solution)/shard_map/all_to_all | solution.py:23
  24.5 31.3 %all-to-all-done.1.second_ref = f32[32,72,128]{2,1,0:T(8,128)S(1)} async-done(((f32[32,72,128]{2,1,0:T(8,128)}), f32[32,72,128]{2,1,0:T(8,128)S(1)}, u32[]{:S(2)}, u32[]{:S(2)}) %all-to-all-start.1) | async-done | bytes 1179680 | tf_op jit(solution)/shard_map/all_to_all | solution.py:23
  55.8 0.6 shard_map.111
  56.4 0.8 copy-done.2
  57.2 6.7 %all-to-all-start.2 = ((f32[16,72,128]{2,1,0:T(8,128)}), f32[16,72,128]{2,1,0:T(8,128)S(1)}, u32[]{:S(2)}, u32[]{:S(2)}) async-start(f32[16,72,128]{2,1,0:T(8,128)} %copy-done.2), calls=%async_computation.2 | async-start | bytes 1179648 | tf_op jit(solution)/shard_map/all_to_all | solution.py:23
  63.9 10.5 %all-to-all-done.2.refs_0_ = f32[16,72,128]{2,1,0:T(8,128)S(1)} async-done(((f32[16,72,128]{2,1,0:T(8,128)}), f32[16,72,128]{2,1,0:T(8,128)S(1)}, u32[]{:S(2)}, u32[]{:S(2)}) %all-to-all-start.2) | async-done | bytes 589856 | tf_op jit(solution)/shard_map/all_to_all | solution.py:23
  74.4 3.7 %shard_map.112 = (f32[16,24,128]{2,1,0:T(8,128)S(1)}, f32[48,128]{1,0:T(8,128)S(1)}, f32[2,48,1024]{2,1,0:T(8,128)S(1)}, f32[16,128]{1,0:T(8,128)S(1)}) custom-call(f32[16,72,128]{2,1,0:T(8,128)S(1)} %all-to-all-done.2.refs_0_, f32[16,128]{1,0:T(8,128)S(1)} %pad.4.refs_1_, f32[48,128]{1,0:T(8,128)S(1)} %constant_dynamic-slice_fusion.1.refs_2_.b_ref), custom_call_target="tpu_custom_call" | custom-call | tf_op jit(solution)/shard_map/pallas_call | solution.py:36
  78.1 10.3 %all_to_all.66.x1_ref = f32[16,24,128]{2,1,0:T(8,128)S(1)} all-to-all(f32[16,24,128]{2,1,0:T(8,128)S(1)} %get-tuple-element.41), channel_id=1, replica_groups=mesh['y'=8,'zh'=4,'co'=2,'zl'=2,'x'=4] {'zl','x','co'}, dimensions={0} | all-to-all | bytes 393216 | tf_op jit(solution)/shard_map/all_to_all | solution.py:23
  88.5 0.3 shard_map.113
  88.8 21.6 %all_to_all.67.x2_ref = f32[32,24,128]{2,1,0:T(8,128)S(1)} all-to-all(f32[32,24,128]{2,1,0:T(8,128)S(1)} %get-tuple-element.44), channel_id=1, replica_groups=mesh['y'=8,'zh'=4,'co'=2,'zl'=2,'x'=4] {'y','zh'}, dimensions={0} | all-to-all | bytes 786432 | tf_op jit(solution)/shard_map/all_to_all | solution.py:23
  110.4 0.7 shard_map.114
  111.1 11.0 %all_to_all.68.x3_ref = f32[16,8,128]{2,1,0:T(8,128)S(1)} all-to-all(f32[16,8,128]{2,1,0:T(8,128)S(1)} %get-tuple-element.47), channel_id=1, replica_groups=mesh['y'=8,'zh'=4,'co'=2,'zl'=2,'x'=4] {'zl','x','co'}, dimensions={0} | all-to-all | bytes 131072 | tf_op jit(solution)/shard_map/all_to_all | solution.py:23
  122.3 16.1 %all_to_all.69.x4_ref = f32[32,8,128]{2,1,0:T(8,128)S(1)} all-to-all(f32[32,8,128]{2,1,0:T(8,128)S(1)} %get-tuple-element.50), channel_id=1, replica_groups=mesh['y'=8,'zh'=4,'co'=2,'zl'=2,'x'=4] {'y','zh'}, dimensions={0} | all-to-all | bytes 262144 | tf_op jit(solution)/shard_map/all_to_all | solution.py:23
  138.5 0.8 shard_map.116
  139.3 10.6 %all_to_all.70.refs_0_ = f32[16,16,128]{2,1,0:T(8,128)S(1)} all-to-all(f32[16,16,128]{2,1,0:T(8,128)S(1)} %get-tuple-element.53), channel_id=1, replica_groups=mesh['y'=8,'zh'=4,'co'=2,'zl'=2,'x'=4] {'zl','x','co'}, dimensions={0} | all-to-all | bytes 262144 | tf_op jit(solution)/shard_map/all_to_all | solution.py:23
  149.9 3.7 %shard_map.117 = (f32[16,24,128]{2,1,0:T(8,128)S(1)}, f32[48,128]{1,0:T(8,128)S(1)}) custom-call(f32[16,16,128]{2,1,0:T(8,128)S(1)} %all_to_all.70.refs_0_, f32[16,128]{1,0:T(8,128)S(1)} %get-tuple-element.54.refs_1_.ec_ref, f32[48,128]{1,0:T(8,128)S(1)} %get-tuple-element.55.refs_2_.b_ref, f32[2,48,1024]{2,1,0:T(8,128)S(1)} %get-tuple-element.56.refs_3_), custom_call_target="tpu_custom_call" | custom-call | tf_op jit(solution)/shard_map/pallas_call | solution.py:36
  153.6 9.8 %all_to_all.71.x1_ref = f32[16,24,128]{2,1,0:T(8,128)S(1)} all-to-all(f32[16,24,128]{2,1,0:T(8,128)S(1)} %get-tuple-element.57), channel_id=1, replica_groups=mesh['y'=8,'zh'=4,'co'=2,'zl'=2,'x'=4] {'zl','x','co'}, dimensions={0} | all-to-all | bytes 393216 | tf_op jit(solution)/shard_map/all_to_all | solution.py:23
  163.8 17.7 %all_to_all.72.x2_ref = f32[32,24,128]{2,1,0:T(8,128)S(1)} all-to-all(f32[32,24,128]{2,1,0:T(8,128)S(1)} %get-tuple-element.60), channel_id=1, replica_groups=mesh['y'=8,'zh'=4,'co'=2,'zl'=2,'x'=4] {'y','zh'}, dimensions={0} | all-to-all | bytes 786432 | tf_op jit(solution)/shard_map/all_to_all | solution.py:23
  181.5 0.7 shard_map.119
  182.1 11.0 %all_to_all.73.x3_ref = f32[16,8,128]{2,1,0:T(8,128)S(1)} all-to-all(f32[16,8,128]{2,1,0:T(8,128)S(1)} %get-tuple-element.63), channel_id=1, replica_groups=mesh['y'=8,'zh'=4,'co'=2,'zl'=2,'x'=4] {'zl','x','co'}, dimensions={0} | all-to-all | bytes 131072 | tf_op jit(solution)/shard_map/all_to_all | solution.py:23
  193.4 16.1 %all_to_all.74.x4_ref = f32[32,8,128]{2,1,0:T(8,128)S(1)} all-to-all(f32[32,8,128]{2,1,0:T(8,128)S(1)} %get-tuple-element.65), channel_id=1, replica_groups=mesh['y'=8,'zh'=4,'co'=2,'zl'=2,'x'=4] {'y','zh'}, dimensions={0} | all-to-all | bytes 262144 | tf_op jit(solution)/shard_map/all_to_all | solution.py:23
  209.5 1.7 shard_map.121
  211.3 5.4 %all-to-all-start.12 = ((f32[16,96,128]{2,1,0:T(8,128)}), f32[16,96,128]{2,1,0:T(8,128)S(1)}, u32[]{:S(2)}, u32[]{:S(2)}) async-start(f32[16,96,128]{2,1,0:T(8,128)} %get-tuple-element.68), calls=%async_computation.12 | async-start | bytes 1572864 | tf_op jit(solution)/shard_map/all_to_all | solution.py:23
  216.8 0.7 copy.16
  217.4 0.6 slice_bitcast_fusion
  218.0 0.6 constant_dynamic-slice_fusion
  218.6 11.1 %all-to-all-done.12.x5_ref = f32[16,96,128]{2,1,0:T(8,128)S(1)} async-done(((f32[16,96,128]{2,1,0:T(8,128)}), f32[16,96,128]{2,1,0:T(8,128)S(1)}, u32[]{:S(2)}, u32[]{:S(2)}) %all-to-all-start.12) | async-done | bytes 786464 | tf_op jit(solution)/shard_map/all_to_all | solution.py:23
  229.7 2.2 shard_map.122
  (22 shorter events, 1.3 us)
Async XLA Ops:
  0.6 63.3 %copy-start = (f32[768,128]{1,0:T(8,128)S(1)}, f32[768,128]{1,0:T(8,128)}, u32[]{:S(2)}) copy-start(f32[768,128]{1,0:T(8,128)} %param.8) | copy-start | bytes 1179652
  0.7 1.0 copy-start.3
  1.7 0.7 copy-start.4
  13.7 10.5 %copy-start.6 = (f32[4,8]{1,0:T(4,128)S(1)}, f32[4,8]{1,0:T(4,128)}, u32[]{:S(2)}) copy-start(f32[4,8]{1,0:T(4,128)} %param.10) | copy-start | bytes 388
  13.7 42.0 %copy-start.1 = (f32[4,32,1,768]{3,2,1,0:T(1,128)S(1)}, f32[4,32,1,768]{3,2,1,0:T(1,128)}, u32[]{:S(2)}) copy-start(f32[4,32,1,768]{3,2,1,0:T(1,128)} %param.6) | copy-start | bytes 1179652
  13.7 42.0 %all-to-all-start.1 = ((f32[32,72,128]{2,1,0:T(8,128)}), f32[32,72,128]{2,1,0:T(8,128)S(1)}, u32[]{:S(2)}, u32[]{:S(2)}) async-start(f32[32,72,128]{2,1,0:T(8,128)} %shard_map.110), calls=%async_computation.1 | async-start | bytes 2359296 | tf_op jit(solution)/shard_map/all_to_all | solution.py:23
  55.8 8.1 %copy-start.5 = (f32[32,16]{0,1:T(8,128)S(1)}, f32[32,16]{0,1:T(8,128)}, u32[]{:S(2)}) copy-start(f32[32,16]{0,1:T(8,128)} %param.9) | copy-start | bytes 6148
  56.4 0.8 copy-start.2
  57.2 17.2 %all-to-all-start.2 = ((f32[16,72,128]{2,1,0:T(8,128)}), f32[16,72,128]{2,1,0:T(8,128)S(1)}, u32[]{:S(2)}, u32[]{:S(2)}) async-start(f32[16,72,128]{2,1,0:T(8,128)} %copy-done.2), calls=%async_computation.2 | async-start | bytes 1179648 | tf_op jit(solution)/shard_map/all_to_all | solution.py:23
  211.3 18.4 %all-to-all-start.12 = ((f32[16,96,128]{2,1,0:T(8,128)}), f32[16,96,128]{2,1,0:T(8,128)S(1)}, u32[]{:S(2)}, u32[]{:S(2)}) async-start(f32[16,96,128]{2,1,0:T(8,128)} %get-tuple-element.68), calls=%async_computation.12 | async-start | bytes 1572864 | tf_op jit(solution)/shard_map/all_to_all | solution.py:23

commit v2 on v1

v2 whole, which is shorter than its diff:
```python
import functools

import jax
import jax.numpy as jnp
from jax import lax
from jax.experimental import pallas as pl
from jax.experimental.pallas import tpu as pltpu
from jax.sharding import Mesh, PartitionSpec as P

STEPS = 2
ETA = 0.2
EPS = 1e-06
SCALE = float(256 * 128 * 16 * 8) ** (-0.5)

FAR = ("y", "zh")
NEAR = ("zl", "x", "co")
NF, NN = 32, 16
PACK_MIB = 56
HIGH, FULL = lax.Precision.HIGH, lax.Precision.HIGHEST
f32 = jnp.float32


def swap(x, axes):
    return lax.all_to_all(x, axes, 0, 0, tiled=True)


def dg(a, b, ca, cb, precision=HIGH):
    return lax.dot_general(a, b, (((ca,), (cb,)), ((), ())), precision=precision, preferred_element_type=f32)


def rate(total, count):
    return ETA * lax.rsqrt(total / count + EPS)


def call(body, outs, *ins, smem=0, hbm=0, scratch=(), mib=10):
    spaces = [pltpu.SMEM] * smem + [pltpu.HBM] * hbm + [pltpu.VMEM] * (len(ins) - smem - hbm)
    specs = [pl.BlockSpec(memory_space=space) for space in spaces]
    return pl.pallas_call(
        body,
        out_shape=[jax.ShapeDtypeStruct(s, f32) for s in outs],
        in_specs=specs,
        out_specs=[pl.BlockSpec(memory_space=pltpu.VMEM)] * len(outs),
        scratch_shapes=list(scratch),
        compiler_params=pltpu.CompilerParams(vmem_limit_bytes=mib * 1024 * 1024),
    )(*ins)


def chosen(rows, lanes, kind, start=0):
    r = lax.broadcasted_iota(jnp.int32, (rows, lanes), 0)
    n = lax.broadcasted_iota(jnp.int32, (rows, lanes), 1)
    n = n // 32 + start if kind == "h" else n % 32
    return jnp.where(r == n, 1.0, 0.0).astype(f32)


def hour_lanes(tm):
    r = lax.broadcasted_iota(jnp.int32, (4, 128), 0)
    n = lax.broadcasted_iota(jnp.int32, (4, 128), 1)
    return jnp.where(n == r + 32 + 4 * tm, 1.0, 0.0).astype(f32)


def expanded(ec_t, lanes, start=0):
    ce = dg(ec_t[:, :32], chosen(32, lanes, "v"), 1, 0, FULL)
    ee = dg(ec_t[:8, 32:64], chosen(32, lanes, "h", start), 1, 0, FULL)
    return ee, ce, (ee[:, None, :] * ce[None, :, :]).reshape(128, lanes)


def residual_body(first, tm_ref, *refs):
    tm = tm_ref[0]
    if first:
        near_ref, b_ref, w_ref, obs_ref, c_ref, e_ref, x1_ref, own_ref, ec_out = refs
        b = b_ref[...]
        own_ref[...] = b_ref[pl.ds(pl.multiple_of(48 * near_ref[0], 8), 48), :]
        e = dg(e_ref[...], hour_lanes(tm), 0, 0, FULL)
        ec_out[...] = jnp.concatenate([e, jnp.zeros((8, 128), f32)], axis=0)
        ec_out[:, 0:32] = c_ref[...]
        ec_t = ec_out[...]
    else:
        w_ref, obs_ref, ec_ref, x1_ref = refs
        b = w_ref[:, 8:56, :].reshape(768, 128)
        ec_t = ec_ref[...]
    w = w_ref[:, 0:8, :].reshape(128, 128)
    ee, ce, ec = expanded(ec_t, 128, 4 * tm)
    q = dg(ec.T, w, 1, 0)
    obs = jnp.concatenate([obs_ref[pl.ds(j, 128, stride=6), :] for j in range(6)], axis=1)
    res = SCALE * dg(q, b, 1, 1) - obs
    x1_ref[:, 16:64, :] = (SCALE * dg(res.T, q, 1, 0)).reshape(16, 48, 128)
    up = SCALE * dg(res, b, 1, 0)
    x1_ref[:, 0:8, :] = dg(ec, up, 1, 0).reshape(16, 8, 128)
    x = dg(w, up, 1, 1).reshape(8, 16, 128)
    ge = dg(jnp.sum(x * ce[None], axis=1), chosen(32, 128, "h", 4 * tm), 1, 1, FULL)
    gc = dg(jnp.sum(x * ee[:, None], axis=0), chosen(32, 128, "v"), 1, 1, FULL)
    x1_ref[:, 8:16, :] = jnp.zeros((16, 8, 128), f32)
    for r in range(16):
        x1_ref[r, 8:9, 0:32] = gc[r : r + 1]
        if r < 8:
            x1_ref[r, 8:9, 32:64] = ge[r : r + 1]


def products(a_ref, far, core):
    a_two = jnp.concatenate([a_ref[pl.ds(far, 1), :], a_ref[pl.ds(far + 32, 1), :]], axis=0)
    top, low = [], []
    for g in core:
        w = dg(a_two, g, 1, 1)
        top.append(w[0:1])
        low.append(w[1:2])
    return jnp.concatenate(top + low, axis=0)


def near_sum_body(x1_ref, core_ref, x2_ref, ga_ref):
    p = []
    for l in range(2):
        t = x1_ref[l, 0:8, :]
        for k in range(1, 8):
            t = t + x1_ref[2 * k + l, 0:8, :]
        p.append(t)
    s = jnp.sum(x1_ref[:, 8:16, :], axis=0)
    gb = jnp.sum(x1_ref[:, 16:64, :], axis=0)
    s = jnp.concatenate(p + [jnp.zeros((8, 128), f32), s], axis=0)
    acc = None
    for c in range(8):
        p = jnp.concatenate([s[c : c + 1], s[8 + c : 9 + c]], axis=0)
        x2_ref[:, :, 128 * c : 128 * c + 128] = jnp.broadcast_to(p[None], (32, 2, 128))
        t = dg(p, core_ref[c], 1, 0)
        acc = t if acc is None else acc + t
    ga_ref[...] = jnp.concatenate([acc[:, :128], acc[:, 128:], jnp.zeros((4, 128), f32)], axis=0)
    tail = jnp.concatenate([s[24:25], jnp.zeros((1, 128), f32)], axis=0)
    x2_ref[:, :, 1152:1280] = jnp.broadcast_to(tail[None], (32, 2, 128))
    x2_ref[:, :, 1024:1152] = jnp.zeros((32, 2, 128), f32)
    for k in range(24):
        x2_ref[k, :, 1024:1152] = gb[2 * k : 2 * k + 2]


def core_grad_body(x2_ref, a_ref, ga_ref, x3_ref, g_ref, gb_ref):
    a = a_ref[...]
    sq = jnp.zeros((1, 128), f32)
    for c in range(8):
        p = jnp.concatenate([x2_ref[:, l, 128 * c : 128 * c + 128] for l in range(2)], axis=0)
        g = dg(p.T, a, 1, 0)
        g_ref[c] = g
        s = jnp.sum(g * g, axis=0, keepdims=True)
        sq = sq + s[:, :128] + s[:, 128:]
    gb = jnp.sum(x2_ref[:, :, 1024:1152], axis=0)
    s = jnp.sum(x2_ref[:, :, 1152:1280], axis=0)
    gb_ref[...] = jnp.concatenate([gb, jnp.zeros((6, 128), f32)], axis=0)
    rows = jnp.concatenate(
        [ga_ref[0:4], s[0:1], sq, jnp.sum(gb * gb, axis=0, keepdims=True), jnp.zeros((1, 128), f32)], axis=0
    )
    x3_ref[...] = jnp.broadcast_to(rows[None], (16, 8, 128))


def near_update_body(x3_ref, gb_ref, ec_ref, x4_ref, new_ref, sq_ref):
    s = jnp.sum(x3_ref[...], axis=0)
    g = x3_ref[:, 4, :]
    lane = lax.broadcasted_iota(jnp.int32, (16, 128), 1)
    gc = jnp.where(lane < 32, g, 0.0)
    ge = jnp.where(jnp.logical_and(lane >= 32, lane < 64), g, 0.0)
    new_ref[...] = ec_ref[...] - rate(jnp.sum(gc * gc), 512.0) * gc - rate(jnp.sum(ge * ge), 256.0) * ge
    sq_ref[...] = jnp.broadcast_to(jnp.sum(s[5:6], axis=1, keepdims=True), (8, 128))
    rows = jnp.concatenate([s[0:4], gb_ref[0:2], s[6:7], jnp.zeros((1, 128), f32)], axis=0)
    x4_ref[...] = jnp.broadcast_to(rows[None], (32, 8, 128))


def far_update_body(last, far_ref, x4_ref, a_ref, b_ref, core_ref, g_ref, sq_ref, x5_ref, a_new, *rest):
    ga = jnp.concatenate(
        [
            jnp.concatenate([x4_ref[:, 0, :], x4_ref[:, 1, :]], axis=0),
            jnp.concatenate([x4_ref[:, 2, :], x4_ref[:, 3, :]], axis=0),
        ],
        axis=1,
    )
    a_new[...] = a_ref[...] - rate(jnp.sum(ga * ga), 16384.0) * ga
    rb = rate(jnp.sum(x4_ref[:, 6, :]), 98304.0)
    gb = jnp.concatenate([x4_ref[k, 4:6, :] for k in range(24)], axis=0)
    b_new = b_ref[...] - rb * gb
    far = far_ref[0]
    rg = ETA * lax.rsqrt(sq_ref[0:1, 0:1] * (1.0 / 4194304) + EPS)
    core = [core_ref[c] - rg * g_ref[c] for c in range(8)]
    w = products(a_new, far, core)
    for k in range(16):
        x5_ref[k, 0:8, :] = w[8 * (k % 2) : 8 * (k % 2) + 8]
    x5_ref[:, 8:56, :] = jnp.broadcast_to(b_new[None], (16, 48, 128))
    if not last:
        b_out, core_out = rest
        b_out[...] = b_new
        for c in range(8):
            core_out[c] = core[c]
        return
    at = pl.ds(pl.multiple_of(far // 2 * 8, 8), 8)
    own = [[], []]
    for c in range(8):
        v = core_ref[c, at, :] - rg * g_ref[c, at, :]
        v = jnp.where(far % 2 == 0, v[0:4], v[4:8])
        for co in range(2):
            own[co] += [v[2 * co : 2 * co + 2, :128], v[2 * co : 2 * co + 2, 128:]]
    for co in range(2):
        rows = jnp.concatenate(own[co], axis=0)
        for t in range(8):
            x5_ref[2 * t + co, 56:88, :] = rows


def pack_body(tm_ref, core_hbm, a_hbm, out_ref, core_ref, a_ref, sems):
    copies = [
        pltpu.make_async_copy(core_hbm.at[tm_ref[0]], core_ref, sems.at[0]),
        pltpu.make_async_copy(a_hbm, a_ref, sems.at[1]),
    ]
    for copy in copies:
        copy.start()
    for copy in copies:
        copy.wait()
    for co in range(2):
        for j in range(16):
            at = 32 * co + 2 * j
            rows = jnp.broadcast_to(core_ref[at : at + 2, :][None], (32, 2, 128))
            for k in range(32):
                out_ref[2 * k + co, :, 128 * j : 128 * j + 128] = rows[k]
    out_ref[:, :, 2048:2176] = jnp.broadcast_to(a_ref[...][None], (64, 2, 128))


def first_products_body(far_ref, all_ref, x5_ref, core_ref, a_ref):
    for k in range(64):
        for c in range(8):
            core_ref[c, 2 * k : 2 * k + 2, :] = all_ref[k, :, 256 * c : 256 * c + 256]
        for half in range(2):
            at = 32 * (k % 2) + k // 2
            lanes = slice(128 * half, 128 * half + 128)
            a_ref[at : at + 1, lanes] = all_ref[k, half : half + 1, 2048:2176]
    x = products(a_ref, far_ref[0], [core_ref[c] for c in range(8)])
    for k in range(16):
        x5_ref[k] = x[8 * (k % 2) : 8 * (k % 2) + 8]


def final_body(
    tm_ref, co_ref, far_ref, obs_ref, x5_ref, ec_ref, a_ref,
    res_ref, b_ref, core_ref, a_out, c_out, e_out,
):
    tm, co = tm_ref[0], co_ref[0]
    ec_t = ec_ref[...]
    _, _, ec = expanded(ec_t, 128, 4 * tm)
    w = x5_ref[:, 0:8, :].reshape(128, 128)
    b = x5_ref[:, 8:56, :].reshape(768, 128)
    b_ref[...] = b
    core_ref[...] = x5_ref[:, 56:88, :].reshape(512, 128)
    q = dg(ec.T, w, 1, 0)
    for j in range(6):
        at = pl.ds(j, 128, stride=6)
        res_ref[at, :] = SCALE * dg(q, b[128 * j : 128 * j + 128], 1, 1) - obs_ref[at, :]
    a_out[...] = a_ref[pl.ds(far_ref[0] + 32 * co, 1), :]
    c_out[...] = ec_t[:, 0:32]
    e_out[...] = dg(hour_lanes(tm), ec_t[0:8], 1, 1, FULL)


def shards(observations, a_factor, b_factor, c_factor, e_factor, core):
    tm = (lax.axis_index("zl") * 4 + lax.axis_index("x")).astype(jnp.int32).reshape(1)
    co = lax.axis_index("co").astype(jnp.int32).reshape(1)
    far = (lax.axis_index("y") * 4 + lax.axis_index("zh")).astype(jnp.int32).reshape(1)

    near = 2 * tm + co

    rows = core.reshape(8, 16, 2, 2, 128).transpose(0, 1, 3, 2, 4).reshape(8, 64, 128)
    obs = observations.reshape(768, 128)
    (first,) = call(
        pack_body,
        [(64, 2, 2176)],
        tm, rows, a_factor.reshape(2, 128),
        smem=1, hbm=2, mib=PACK_MIB,
        scratch=(pltpu.VMEM((64, 128), f32), pltpu.VMEM((2, 128), f32), pltpu.SemaphoreType.DMA((2,))),
    )
    x5, core_part, a_all = call(
        first_products_body,
        [(16, 8, 128), (8, 128, 256), (64, 256)],
        far, swap(first, FAR + ("co",)),
        smem=1,
    )
    x5 = swap(x5, NEAR)

    for step in range(STEPS):
        last = step == STEPS - 1
        if step == 0:
            x1, b_part, ec_t = call(
                functools.partial(residual_body, True),
                [(16, 64, 128), (48, 128), (16, 128)],
                tm, near, b_factor, x5, obs, c_factor.T, e_factor,
                smem=2,
            )
        else:
            (x1,) = call(functools.partial(residual_body, False), [(16, 64, 128)], tm, x5, obs, ec_t, smem=1)
        x2, ga = call(near_sum_body, [(32, 2, 1280), (8, 128)], swap(x1, NEAR), core_part)
        x3, g_core, gb = call(core_grad_body, [(16, 8, 128), (8, 128, 256), (8, 128)], swap(x2, FAR), a_all, ga)
        x4, ec_t, sq = call(near_update_body, [(32, 8, 128), (16, 128), (8, 128)], swap(x3, NEAR), gb, ec_t)
        more = [] if last else [(48, 128), (8, 128, 256)]
        x5, a_all, *rest = call(
            functools.partial(far_update_body, last),
            [(16, 88 if last else 56, 128), (64, 256)] + more,
            far, swap(x4, FAR), a_all, b_part, core_part, g_core, sq,
            smem=1,
        )
        x5 = swap(x5, NEAR)
        if not last:
            b_part, core_part = rest

    residual, b_new, core_new, a_new, c_new, e_new = call(
        final_body,
        [(768, 128), (768, 128), (512, 128), (1, 256), (16, 32), (4, 8)],
        tm, co, far, obs, x5, ec_t, a_all,
        smem=3,
    )
    core_new = core_new.reshape(8, 16, 2, 2, 128).transpose(0, 1, 3, 2, 4).reshape(8, 16, 2, 256)
    return (residual.reshape(4, 32, 1, 768), a_new, b_new, c_new.T, e_new, core_new)


def solution(mesh):
    fine = Mesh(mesh.devices.reshape(8, 4, 2, 2, 4), ("y", "zh", "co", "zl", "x"))
    grid, tm = ("y", "zh", "co"), ("zl", "x")
    specs = (P(tm, None, grid, None), P(grid, None), P(), P(), P(tm, None), P(None, None, grid, None))
    return jax.shard_map(shards, mesh=fine, in_specs=specs, out_specs=specs, check_vma=False)
```

time: 233 us -> 222 us (0.953)
  waiting for transfers between devices: 52.9 us -> 36.2 us
  blocking collectives: 135 us -> 147 us
  local copies, waits for them, and re-layouts: 4.73 us -> 0.03 us
  Pallas kernels: 16.4 us -> 13.2 us
    all_to_all x3 -> x2, waiting for transfers between devices: 52.9 us -> 36.2 us  [swap(): return lax.all_to_all(x, axes, 0, 0, tiled=True)]
    all_to_all x10, blocking collectives: 135 us -> 147 us  [swap(): return lax.all_to_all(x, axes, 0, 0, tiled=True)]
    unnamed x16 -> x8, local copies, waits for them, and re-layouts: 3.25 us -> 0.03 us
    pallas_call x14 -> x13, Pallas kernels: 16.4 us -> 13.2 us  [call(): pl.pallas_call(body, out_shape=[jax.ShapeDtypeStruct(s, f32) for s in out...]
    all_to_all x3 -> x2, starting transfers between devices: 22.5 us -> 24.2 us  [swap(): return lax.all_to_all(x, axes, 0, 0, tiled=True)]
  transfers between devices with their start and end apart: 3 -> 2, of which waited for: 3 -> 2; matrix products, arithmetic and copies ran while one was open for 1% -> 0% of each run, Pallas kernels for 0% -> 0%
where the time goes in v2:
time: 222 us; the launch traced here: 221 us
  blocking collectives  147 us (66%)
  waiting for transfers between devices  36.2 us (16%)
  starting transfers between devices  24.2 us (11%)
  Pallas kernels  13.2 us (6%)
    all_to_all x10, blocking collectives, swap(): return lax.all_to_all(x, axes, 0, 0, tiled=True)  147 us
    all_to_all x2, waiting for transfers between devices, swap(): return lax.all_to_all(x, axes, 0, 0, tiled=True)  36.2 us
    all_to_all x2, starting transfers between devices, swap(): return lax.all_to_all(x, axes, 0, 0, tiled=True)  24.2 us
    pallas_call x13, Pallas kernels, call(): pl.pallas_call(body, out_shape=[jax.ShapeDtypeStruct(s, f32) for s in out...  13.2 us
  transfers between devices with their start and end apart: 2, of which 2 were waited for; matrix products, arithmetic and copies ran while one was open for 0% of the time, Pallas kernels for 0%

profile of v2, /device:TPU:1, one launch (start us, length us, event | category | flops | bytes accessed | tf_op | source)
XLA Modules:
  0.0 221.3 jit_solution(2324153352631257644)
XLA Ops:
  0.6 2.1 shard_map.109
  2.7 17.6 %all-to-all-start = ((f32[64,2,2176]{2,1,0:T(2,128)}), f32[64,2,2176]{2,1,0:T(2,128)S(1)}, u32[]{:S(2)}, u32[]{:S(2)}) async-start(f32[64,2,2176]{2,1,0:T(2,128)} %shard_map.109), calls=%async_computation | async-start | bytes 2228224 | tf_op jit(solution)/shard_map/all_to_all | solution.py:24
  20.4 0.0 copy-start
  20.4 0.0 copy-start.1
  20.4 0.0 copy-start.2
  20.4 0.0 copy-start.3
  20.4 30.4 %all-to-all-done.all_ref = f32[64,2,2176]{2,1,0:T(2,128)S(1)} async-done(((f32[64,2,2176]{2,1,0:T(2,128)}), f32[64,2,2176]{2,1,0:T(2,128)S(1)}, u32[]{:S(2)}, u32[]{:S(2)}) %all-to-all-start) | async-done | bytes 1114144 | tf_op jit(solution)/shard_map/all_to_all | solution.py:24
  50.8 1.4 shard_map.110
  52.2 6.6 %all-to-all-start.1 = ((f32[16,8,128]{2,1,0:T(8,128)}), f32[16,8,128]{2,1,0:T(8,128)S(1)}, u32[]{:S(2)}, u32[]{:S(2)}) async-start(f32[16,8,128]{2,1,0:T(8,128)} %get-tuple-element.40), calls=%async_computation.1 | async-start | bytes 131072 | tf_op jit(solution)/shard_map/all_to_all | solution.py:24
  58.8 5.8 %all-to-all-done.1.refs_2_ = f32[16,8,128]{2,1,0:T(8,128)S(1)} async-done(((f32[16,8,128]{2,1,0:T(8,128)}), f32[16,8,128]{2,1,0:T(8,128)S(1)}, u32[]{:S(2)}, u32[]{:S(2)}) %all-to-all-start.1) | async-done | bytes 65568 | tf_op jit(solution)/shard_map/all_to_all | solution.py:24
  64.6 0.0 copy-done
  64.6 1.9 shard_map.111
  66.6 12.8 %all_to_all.60.x1_ref = f32[16,64,128]{2,1,0:T(8,128)S(1)} all-to-all(f32[16,64,128]{2,1,0:T(8,128)S(1)} %get-tuple-element.41), channel_id=1, replica_groups=mesh['y'=8,'zh'=4,'co'=2,'zl'=2,'x'=4] {'zl','x','co'}, dimensions={0} | all-to-all | bytes 1048576 | tf_op jit(solution)/shard_map/all_to_all | solution.py:24
  79.3 0.4 shard_map.112
  79.7 18.2 %all_to_all.61.x2_ref = f32[32,2,1280]{2,1,0:T(2,128)S(1)} all-to-all(f32[32,2,1280]{2,1,0:T(2,128)S(1)} %get-tuple-element.43), channel_id=1, replica_groups=mesh['y'=8,'zh'=4,'co'=2,'zl'=2,'x'=4] {'y','zh'}, dimensions={0} | all-to-all | bytes 655360 | tf_op jit(solution)/shard_map/all_to_all | solution.py:24
  98.0 0.7 shard_map.113
  98.6 12.5 %all_to_all.62.x3_ref = f32[16,8,128]{2,1,0:T(8,128)S(1)} all-to-all(f32[16,8,128]{2,1,0:T(8,128)S(1)} %get-tuple-element.46), channel_id=1, replica_groups=mesh['y'=8,'zh'=4,'co'=2,'zl'=2,'x'=4] {'zl','x','co'}, dimensions={0} | all-to-all | bytes 131072 | tf_op jit(solution)/shard_map/all_to_all | solution.py:24
  111.2 0.2 shard_map.114
  111.4 15.7 %all_to_all.63.x4_ref = f32[32,8,128]{2,1,0:T(8,128)S(1)} all-to-all(f32[32,8,128]{2,1,0:T(8,128)S(1)} %get-tuple-element.49), channel_id=1, replica_groups=mesh['y'=8,'zh'=4,'co'=2,'zl'=2,'x'=4] {'y','zh'}, dimensions={0} | all-to-all | bytes 262144 | tf_op jit(solution)/shard_map/all_to_all | solution.py:24
  127.1 0.9 shard_map.115
  128.0 13.6 %all_to_all.64.refs_0_ = f32[16,56,128]{2,1,0:T(8,128)S(1)} all-to-all(f32[16,56,128]{2,1,0:T(8,128)S(1)} %get-tuple-element.53), channel_id=1, replica_groups=mesh['y'=8,'zh'=4,'co'=2,'zl'=2,'x'=4] {'zl','x','co'}, dimensions={0} | all-to-all | bytes 917504 | tf_op jit(solution)/shard_map/all_to_all | solution.py:24
  141.6 1.7 shard_map.116
  143.3 13.5 %all_to_all.65.x1_ref = f32[16,64,128]{2,1,0:T(8,128)S(1)} all-to-all(f32[16,64,128]{2,1,0:T(8,128)S(1)} %shard_map.116), channel_id=1, replica_groups=mesh['y'=8,'zh'=4,'co'=2,'zl'=2,'x'=4] {'zl','x','co'}, dimensions={0} | all-to-all | bytes 1048576 | tf_op jit(solution)/shard_map/all_to_all | solution.py:24
  156.8 0.4 shard_map.117
  157.2 15.6 %all_to_all.66.x2_ref = f32[32,2,1280]{2,1,0:T(2,128)S(1)} all-to-all(f32[32,2,1280]{2,1,0:T(2,128)S(1)} %get-tuple-element.56), channel_id=1, replica_groups=mesh['y'=8,'zh'=4,'co'=2,'zl'=2,'x'=4] {'y','zh'}, dimensions={0} | all-to-all | bytes 655360 | tf_op jit(solution)/shard_map/all_to_all | solution.py:24
  172.8 0.7 shard_map.118
  173.5 12.5 %all_to_all.67.x3_ref = f32[16,8,128]{2,1,0:T(8,128)S(1)} all-to-all(f32[16,8,128]{2,1,0:T(8,128)S(1)} %get-tuple-element.59), channel_id=1, replica_groups=mesh['y'=8,'zh'=4,'co'=2,'zl'=2,'x'=4] {'zl','x','co'}, dimensions={0} | all-to-all | bytes 131072 | tf_op jit(solution)/shard_map/all_to_all | solution.py:24
  186.1 0.2 shard_map.119
  186.3 15.7 %all_to_all.68.x4_ref = f32[32,8,128]{2,1,0:T(8,128)S(1)} all-to-all(f32[32,8,128]{2,1,0:T(8,128)S(1)} %get-tuple-element.61), channel_id=1, replica_groups=mesh['y'=8,'zh'=4,'co'=2,'zl'=2,'x'=4] {'y','zh'}, dimensions={0} | all-to-all | bytes 262144 | tf_op jit(solution)/shard_map/all_to_all | solution.py:24
  202.0 0.9 shard_map.120
  202.9 16.8 %all_to_all.69.x5_ref = f32[16,88,128]{2,1,0:T(8,128)S(1)} all-to-all(f32[16,88,128]{2,1,0:T(8,128)S(1)} %get-tuple-element.65), channel_id=1, replica_groups=mesh['y'=8,'zh'=4,'co'=2,'zl'=2,'x'=4] {'zl','x','co'}, dimensions={0} | all-to-all | bytes 1441792 | tf_op jit(solution)/shard_map/all_to_all | solution.py:24
  219.6 1.7 shard_map.121
  (3 shorter events, 0.0 us)
Async XLA Ops:
  2.7 48.1 %all-to-all-start = ((f32[64,2,2176]{2,1,0:T(2,128)}), f32[64,2,2176]{2,1,0:T(2,128)S(1)}, u32[]{:S(2)}, u32[]{:S(2)}) async-start(f32[64,2,2176]{2,1,0:T(2,128)} %shard_map.109), calls=%async_computation | async-start | bytes 2228224 | tf_op jit(solution)/shard_map/all_to_all | solution.py:24
  20.4 44.3 %copy-start = (f32[4,32,1,768]{3,2,1,0:T(1,128)S(1)}, f32[4,32,1,768]{3,2,1,0:T(1,128)}, u32[]{:S(2)}) copy-start(f32[4,32,1,768]{3,2,1,0:T(1,128)} %param.6) | copy-start | bytes 1179652
  20.4 44.2 %copy-start.1 = (f32[768,128]{1,0:T(8,128)S(1)}, f32[768,128]{1,0:T(8,128)}, u32[]{:S(2)}) copy-start(f32[768,128]{1,0:T(8,128)} %refs_1_.1) | copy-start | bytes 1179652
  20.4 44.2 %copy-start.2 = (f32[32,16]{0,1:T(8,128)S(1)}, f32[32,16]{0,1:T(8,128)}, u32[]{:S(2)}) copy-start(f32[32,16]{0,1:T(8,128)} %param.9) | copy-start | bytes 6148
  20.4 44.2 %copy-start.3 = (f32[4,8]{1,0:T(4,128)S(1)}, f32[4,8]{1,0:T(4,128)}, u32[]{:S(2)}) copy-start(f32[4,8]{1,0:T(4,128)} %refs_5_.1) | copy-start | bytes 388
  52.2 12.4 %all-to-all-start.1 = ((f32[16,8,128]{2,1,0:T(8,128)}), f32[16,8,128]{2,1,0:T(8,128)S(1)}, u32[]{:S(2)}, u32[]{:S(2)}) async-start(f32[16,8,128]{2,1,0:T(8,128)} %get-tuple-element.40), calls=%async_computation.1 | async-start | bytes 131072 | tf_op jit(solution)/shard_map/all_to_all | solution.py:24

commit v3 on v2

--- a/solution.py
+++ b/solution.py
@@ -66,34 +66,23 @@
 
 def residual_body(first, tm_ref, *refs):
     tm = tm_ref[0]
-    if first:
-        near_ref, b_ref, w_ref, obs_ref, c_ref, e_ref, x1_ref, own_ref, ec_out = refs
-        b = b_ref[...]
-        own_ref[...] = b_ref[pl.ds(pl.multiple_of(48 * near_ref[0], 8), 48), :]
-        e = dg(e_ref[...], hour_lanes(tm), 0, 0, FULL)
-        ec_out[...] = jnp.concatenate([e, jnp.zeros((8, 128), f32)], axis=0)
-        ec_out[:, 0:32] = c_ref[...]
-        ec_t = ec_out[...]
-    else:
-        w_ref, obs_ref, ec_ref, x1_ref = refs
-        b = w_ref[:, 8:56, :].reshape(768, 128)
-        ec_t = ec_ref[...]
+    w_ref, obs_ref, ec_ref, *b_ref, x1_ref, gec_ref = refs
+    b = b_ref[0][...] if first else w_ref[:, 8:56, :].reshape(768, 128)
+    ec_t = ec_ref[...]
     w = w_ref[:, 0:8, :].reshape(128, 128)
     ee, ce, ec = expanded(ec_t, 128, 4 * tm)
     q = dg(ec.T, w, 1, 0)
     obs = jnp.concatenate([obs_ref[pl.ds(j, 128, stride=6), :] for j in range(6)], axis=1)
     res = SCALE * dg(q, b, 1, 1) - obs
-    x1_ref[:, 16:64, :] = (SCALE * dg(res.T, q, 1, 0)).reshape(16, 48, 128)
+    x1_ref[:, 8:56, :] = (SCALE * dg(res.T, q, 1, 0)).reshape(16, 48, 128)
     up = SCALE * dg(res, b, 1, 0)
     x1_ref[:, 0:8, :] = dg(ec, up, 1, 0).reshape(16, 8, 128)
     x = dg(w, up, 1, 1).reshape(8, 16, 128)
     ge = dg(jnp.sum(x * ce[None], axis=1), chosen(32, 128, "h", 4 * tm), 1, 1, FULL)
     gc = dg(jnp.sum(x * ee[:, None], axis=0), chosen(32, 128, "v"), 1, 1, FULL)
-    x1_ref[:, 8:16, :] = jnp.zeros((16, 8, 128), f32)
-    for r in range(16):
-        x1_ref[r, 8:9, 0:32] = gc[r : r + 1]
-        if r < 8:
-            x1_ref[r, 8:9, 32:64] = ge[r : r + 1]
+    gec_ref[...] = jnp.zeros((16, 128), f32)
+    gec_ref[:, 0:32] = gc
+    gec_ref[0:8, 32:64] = ge
 
 
 def products(a_ref, far, core):
@@ -106,16 +95,15 @@
     return jnp.concatenate(top + low, axis=0)
 
 
-def near_sum_body(x1_ref, core_ref, x2_ref, ga_ref):
+def near_sum_body(x1_ref, gec_ref, core_ref, x2_ref, ga_ref):
     p = []
     for l in range(2):
         t = x1_ref[l, 0:8, :]
         for k in range(1, 8):
             t = t + x1_ref[2 * k + l, 0:8, :]
         p.append(t)
-    s = jnp.sum(x1_ref[:, 8:16, :], axis=0)
-    gb = jnp.sum(x1_ref[:, 16:64, :], axis=0)
-    s = jnp.concatenate(p + [jnp.zeros((8, 128), f32), s], axis=0)
+    gb = jnp.sum(x1_ref[:, 8:56, :], axis=0)
+    s = jnp.concatenate(p, axis=0)
     acc = None
     for c in range(8):
         p = jnp.concatenate([s[c : c + 1], s[8 + c : 9 + c]], axis=0)
@@ -123,14 +111,13 @@
         t = dg(p, core_ref[c], 1, 0)
         acc = t if acc is None else acc + t
     ga_ref[...] = jnp.concatenate([acc[:, :128], acc[:, 128:], jnp.zeros((4, 128), f32)], axis=0)
-    tail = jnp.concatenate([s[24:25], jnp.zeros((1, 128), f32)], axis=0)
-    x2_ref[:, :, 1152:1280] = jnp.broadcast_to(tail[None], (32, 2, 128))
-    x2_ref[:, :, 1024:1152] = jnp.zeros((32, 2, 128), f32)
     for k in range(24):
         x2_ref[k, :, 1024:1152] = gb[2 * k : 2 * k + 2]
-
-
-def core_grad_body(x2_ref, a_ref, ga_ref, x3_ref, g_ref, gb_ref):
+    for k in range(8):
+        x2_ref[24 + k, :, 1024:1152] = gec_ref[2 * k : 2 * k + 2, :]
+
+
+def core_grad_body(far_ref, x2_ref, a_ref, ga_ref, x3_ref, g_ref, gb_ref):
     a = a_ref[...]
     sq = jnp.zeros((1, 128), f32)
     for c in range(8):
@@ -140,27 +127,22 @@
         s = jnp.sum(g * g, axis=0, keepdims=True)
         sq = sq + s[:, :128] + s[:, 128:]
     gb = jnp.sum(x2_ref[:, :, 1024:1152], axis=0)
-    s = jnp.sum(x2_ref[:, :, 1152:1280], axis=0)
     gb_ref[...] = jnp.concatenate([gb, jnp.zeros((6, 128), f32)], axis=0)
-    rows = jnp.concatenate(
-        [ga_ref[0:4], s[0:1], sq, jnp.sum(gb * gb, axis=0, keepdims=True), jnp.zeros((1, 128), f32)], axis=0
-    )
-    x3_ref[...] = jnp.broadcast_to(rows[None], (16, 8, 128))
-
-
-def near_update_body(x3_ref, gb_ref, ec_ref, x4_ref, new_ref, sq_ref):
+    sb = jnp.where(far_ref[0] < 24, jnp.sum(gb * gb, axis=0, keepdims=True), 0.0)
+    x3_ref[...] = jnp.broadcast_to(jnp.concatenate([ga_ref[0:4], gb, sq, sb], axis=0)[None], (16, 8, 128))
+
+
+def near_update_body(far_ref, x3_ref, gb_ref, x4_ref, sq_ref):
     s = jnp.sum(x3_ref[...], axis=0)
-    g = x3_ref[:, 4, :]
-    lane = lax.broadcasted_iota(jnp.int32, (16, 128), 1)
-    gc = jnp.where(lane < 32, g, 0.0)
-    ge = jnp.where(jnp.logical_and(lane >= 32, lane < 64), g, 0.0)
-    new_ref[...] = ec_ref[...] - rate(jnp.sum(gc * gc), 512.0) * gc - rate(jnp.sum(ge * ge), 256.0) * ge
-    sq_ref[...] = jnp.broadcast_to(jnp.sum(s[5:6], axis=1, keepdims=True), (8, 128))
-    rows = jnp.concatenate([s[0:4], gb_ref[0:2], s[6:7], jnp.zeros((1, 128), f32)], axis=0)
+    sq_ref[...] = jnp.broadcast_to(jnp.sum(s[6:7], axis=1, keepdims=True), (8, 128))
+    gb = jnp.where(far_ref[0] < 24, gb_ref[0:2], s[4:6])
+    rows = jnp.concatenate([s[0:4], gb, s[7:8], jnp.zeros((1, 128), f32)], axis=0)
     x4_ref[...] = jnp.broadcast_to(rows[None], (32, 8, 128))
 
 
-def far_update_body(last, far_ref, x4_ref, a_ref, b_ref, core_ref, g_ref, sq_ref, x5_ref, a_new, *rest):
+def far_update_body(
+    last, far_ref, x4_ref, a_ref, b_ref, core_ref, g_ref, sq_ref, ec_ref, x5_ref, a_new, ec_new, *rest
+):
     ga = jnp.concatenate(
         [
             jnp.concatenate([x4_ref[:, 0, :], x4_ref[:, 1, :]], axis=0),
@@ -172,6 +154,11 @@
     rb = rate(jnp.sum(x4_ref[:, 6, :]), 98304.0)
     gb = jnp.concatenate([x4_ref[k, 4:6, :] for k in range(24)], axis=0)
     b_new = b_ref[...] - rb * gb
+    g = jnp.concatenate([x4_ref[24 + k, 4:6, :] for k in range(8)], axis=0)
+    lane = lax.broadcasted_iota(jnp.int32, (16, 128), 1)
+    gc = jnp.where(lane < 32, g, 0.0)
+    ge = jnp.where(jnp.logical_and(lane >= 32, lane < 64), g, 0.0)
+    ec_new[...] = ec_ref[...] - rate(jnp.sum(gc * gc), 512.0) * gc - rate(jnp.sum(ge * ge), 256.0) * ge
     far = far_ref[0]
     rg = ETA * lax.rsqrt(sq_ref[0:1, 0:1] * (1.0 / 4194304) + EPS)
     core = [core_ref[c] - rg * g_ref[c] for c in range(8)]
@@ -216,7 +203,13 @@
     out_ref[:, :, 2048:2176] = jnp.broadcast_to(a_ref[...][None], (64, 2, 128))
 
 
-def first_products_body(far_ref, all_ref, x5_ref, core_ref, a_ref):
+def first_products_body(
+    far_ref, tm_ref, near_ref, all_ref, b_ref, c_ref, e_ref, obs_ref, x5_ref, core_ref, a_ref, own_ref, ec_ref
+):
+    own_ref[...] = b_ref[pl.ds(pl.multiple_of(48 * near_ref[0], 8), 48), :]
+    e = dg(e_ref[...], hour_lanes(tm_ref[0]), 0, 0, FULL)
+    ec_ref[...] = jnp.concatenate([e, jnp.zeros((8, 128), f32)], axis=0)
+    ec_ref[:, 0:32] = c_ref[...]
     for k in range(64):
         for c in range(8):
             core_ref[c, 2 * k : 2 * k + 2, :] = all_ref[k, :, 256 * c : 256 * c + 256]
@@ -265,33 +258,33 @@
         smem=1, hbm=2, mib=PACK_MIB,
         scratch=(pltpu.VMEM((64, 128), f32), pltpu.VMEM((2, 128), f32), pltpu.SemaphoreType.DMA((2,))),
     )
-    x5, core_part, a_all = call(
+    x5, core_part, a_all, b_part, ec_t = call(
         first_products_body,
-        [(16, 8, 128), (8, 128, 256), (64, 256)],
-        far, swap(first, FAR + ("co",)),
-        smem=1,
+        [(16, 8, 128), (8, 128, 256), (64, 256), (48, 128), (16, 128)],
+        far, tm, near, swap(first, FAR + ("co",)), b_factor, c_factor.T, e_factor, obs,
+        smem=3,
     )
     x5 = swap(x5, NEAR)
 
     for step in range(STEPS):
         last = step == STEPS - 1
-        if step == 0:
-            x1, b_part, ec_t = call(
-                functools.partial(residual_body, True),
-                [(16, 64, 128), (48, 128), (16, 128)],
-                tm, near, b_factor, x5, obs, c_factor.T, e_factor,
-                smem=2,
-            )
-        else:
-            (x1,) = call(functools.partial(residual_body, False), [(16, 64, 128)], tm, x5, obs, ec_t, smem=1)
-        x2, ga = call(near_sum_body, [(32, 2, 1280), (8, 128)], swap(x1, NEAR), core_part)
-        x3, g_core, gb = call(core_grad_body, [(16, 8, 128), (8, 128, 256), (8, 128)], swap(x2, FAR), a_all, ga)
-        x4, ec_t, sq = call(near_update_body, [(32, 8, 128), (16, 128), (8, 128)], swap(x3, NEAR), gb, ec_t)
+        begin = [b_factor] if step == 0 else []
+        x1, gec = call(
+            functools.partial(residual_body, step == 0),
+            [(16, 56, 128), (16, 128)],
+            tm, x5, obs, ec_t, *begin,
+            smem=1,
+        )
+        x2, ga = call(near_sum_body, [(32, 2, 1152), (8, 128)], swap(x1, NEAR), gec, core_part)
+        x3, g_core, gb = call(
+            core_grad_body, [(16, 8, 128), (8, 128, 256), (8, 128)], far, swap(x2, FAR), a_all, ga, smem=1
+        )
+        x4, sq = call(near_update_body, [(32, 8, 128), (8, 128)], far, swap(x3, NEAR), gb, smem=1)
         more = [] if last else [(48, 128), (8, 128, 256)]
-        x5, a_all, *rest = call(
+        x5, a_all, ec_t, *rest = call(
             functools.partial(far_update_body, last),
-            [(16, 88 if last else 56, 128), (64, 256)] + more,
-            far, swap(x4, FAR), a_all, b_part, core_part, g_core, sq,
+            [(16, 88 if last else 56, 128), (64, 256), (16, 128)] + more,
+            far, swap(x4, FAR), a_all, b_part, core_part, g_core, sq, ec_t,
             smem=1,
         )
         x5 = swap(x5, NEAR)

time: 222 us -> 218 us (0.982)
  blocking collectives: 147 us -> 156 us
  starting transfers between devices: 24.2 us -> 17.8 us
  waiting for transfers between devices: 36.2 us -> 30.4 us
    all_to_all x10 -> x11, blocking collectives: 147 us -> 156 us  [swap(): return lax.all_to_all(x, axes, 0, 0, tiled=True)]
    all_to_all x2 -> x1, starting transfers between devices: 24.2 us -> 17.8 us  [swap(): return lax.all_to_all(x, axes, 0, 0, tiled=True)]
    all_to_all x2 -> x1, waiting for transfers between devices: 36.2 us -> 30.4 us  [swap(): return lax.all_to_all(x, axes, 0, 0, tiled=True)]
  transfers between devices with their start and end apart: 2 -> 1, of which waited for: 2 -> 1; matrix products, arithmetic and copies ran while one was open for 0% -> 0% of each run, Pallas kernels for 0% -> 0%
where the time goes in v3:
time: 218 us; the launch traced here: 217 us
  blocking collectives  156 us (72%)
  waiting for transfers between devices  30.4 us (14%)
  starting transfers between devices  17.8 us (8%)
  Pallas kernels  12.2 us (6%)
    all_to_all x11, blocking collectives, swap(): return lax.all_to_all(x, axes, 0, 0, tiled=True)  156 us
    all_to_all x1, waiting for transfers between devices, swap(): return lax.all_to_all(x, axes, 0, 0, tiled=True)  30.4 us
    all_to_all x1, starting transfers between devices, swap(): return lax.all_to_all(x, axes, 0, 0, tiled=True)  17.8 us
    pallas_call x13, Pallas kernels, call(): pl.pallas_call(body, out_shape=[jax.ShapeDtypeStruct(s, f32) for s in out...  12.2 us
  transfers between devices with their start and end apart: 1, of which 1 were waited for; matrix products, arithmetic and copies ran while one was open for 0% of the time, Pallas kernels for 0%

profile of v3, /device:TPU:1, one launch (start us, length us, event | category | flops | bytes accessed | tf_op | source)
XLA Modules:
  0.0 217.4 jit_solution(12775155750118447168)
XLA Ops:
  0.6 2.1 shard_map.109
  2.7 0.0 copy-start
  2.7 0.0 copy-start.1
  2.7 0.0 copy-start.2
  2.8 0.0 copy-start.3
  2.8 17.8 %all-to-all-start = ((f32[64,2,2176]{2,1,0:T(2,128)}), f32[64,2,2176]{2,1,0:T(2,128)S(1)}, u32[]{:S(2)}, u32[]{:S(2)}) async-start(f32[64,2,2176]{2,1,0:T(2,128)} %shard_map.109), calls=%async_computation | async-start | bytes 2228224 | tf_op jit(solution)/shard_map/all_to_all | solution.py:24
  20.6 30.4 %all-to-all-done.all_ref = f32[64,2,2176]{2,1,0:T(2,128)S(1)} async-done(((f32[64,2,2176]{2,1,0:T(2,128)}), f32[64,2,2176]{2,1,0:T(2,128)S(1)}, u32[]{:S(2)}, u32[]{:S(2)}) %all-to-all-start) | async-done | bytes 1114144 | tf_op jit(solution)/shard_map/all_to_all | solution.py:24
  51.0 0.0 copy-done
  51.0 0.0 copy-done.1
  51.0 0.8 shard_map.110
  51.8 12.2 %all_to_all.60.refs_0_ = f32[16,8,128]{2,1,0:T(8,128)S(1)} all-to-all(f32[16,8,128]{2,1,0:T(8,128)S(1)} %get-tuple-element.43), channel_id=1, replica_groups=mesh['y'=8,'zh'=4,'co'=2,'zl'=2,'x'=4] {'zl','x','co'}, dimensions={0} | all-to-all | bytes 131072 | tf_op jit(solution)/shard_map/all_to_all | solution.py:24
  64.0 1.7 shard_map.111
  65.7 12.0 %all_to_all.61.x1_ref = f32[16,56,128]{2,1,0:T(8,128)S(1)} all-to-all(f32[16,56,128]{2,1,0:T(8,128)S(1)} %get-tuple-element.45), channel_id=1, replica_groups=mesh['y'=8,'zh'=4,'co'=2,'zl'=2,'x'=4] {'zl','x','co'}, dimensions={0} | all-to-all | bytes 917504 | tf_op jit(solution)/shard_map/all_to_all | solution.py:24
  77.8 0.4 shard_map.112
  78.2 17.4 %all_to_all.62.x2_ref = f32[32,2,1152]{2,1,0:T(2,128)S(1)} all-to-all(f32[32,2,1152]{2,1,0:T(2,128)S(1)} %get-tuple-element.48), channel_id=1, replica_groups=mesh['y'=8,'zh'=4,'co'=2,'zl'=2,'x'=4] {'y','zh'}, dimensions={0} | all-to-all | bytes 589824 | tf_op jit(solution)/shard_map/all_to_all | solution.py:24
  95.5 0.7 shard_map.113
  96.2 12.8 %all_to_all.63.x3_ref = f32[16,8,128]{2,1,0:T(8,128)S(1)} all-to-all(f32[16,8,128]{2,1,0:T(8,128)S(1)} %get-tuple-element.51), channel_id=1, replica_groups=mesh['y'=8,'zh'=4,'co'=2,'zl'=2,'x'=4] {'zl','x','co'}, dimensions={0} | all-to-all | bytes 131072 | tf_op jit(solution)/shard_map/all_to_all | solution.py:24
  109.0 0.1 shard_map.114
  109.1 15.6 %all_to_all.64.x4_ref = f32[32,8,128]{2,1,0:T(8,128)S(1)} all-to-all(f32[32,8,128]{2,1,0:T(8,128)S(1)} %get-tuple-element.53), channel_id=1, replica_groups=mesh['y'=8,'zh'=4,'co'=2,'zl'=2,'x'=4] {'y','zh'}, dimensions={0} | all-to-all | bytes 262144 | tf_op jit(solution)/shard_map/all_to_all | solution.py:24
  124.7 0.9 shard_map.115
  125.6 13.6 %all_to_all.65.refs_0_ = f32[16,56,128]{2,1,0:T(8,128)S(1)} all-to-all(f32[16,56,128]{2,1,0:T(8,128)S(1)} %get-tuple-element.57), channel_id=1, replica_groups=mesh['y'=8,'zh'=4,'co'=2,'zl'=2,'x'=4] {'zl','x','co'}, dimensions={0} | all-to-all | bytes 917504 | tf_op jit(solution)/shard_map/all_to_all | solution.py:24
  139.2 1.7 shard_map.116
  141.0 12.8 %all_to_all.66.x1_ref = f32[16,56,128]{2,1,0:T(8,128)S(1)} all-to-all(f32[16,56,128]{2,1,0:T(8,128)S(1)} %get-tuple-element.59), channel_id=1, replica_groups=mesh['y'=8,'zh'=4,'co'=2,'zl'=2,'x'=4] {'zl','x','co'}, dimensions={0} | all-to-all | bytes 917504 | tf_op jit(solution)/shard_map/all_to_all | solution.py:24
  153.7 0.4 shard_map.117
  154.1 14.7 %all_to_all.67.x2_ref = f32[32,2,1152]{2,1,0:T(2,128)S(1)} all-to-all(f32[32,2,1152]{2,1,0:T(2,128)S(1)} %get-tuple-element.62), channel_id=1, replica_groups=mesh['y'=8,'zh'=4,'co'=2,'zl'=2,'x'=4] {'y','zh'}, dimensions={0} | all-to-all | bytes 589824 | tf_op jit(solution)/shard_map/all_to_all | solution.py:24
  168.8 0.7 shard_map.118
  169.5 12.8 %all_to_all.68.x3_ref = f32[16,8,128]{2,1,0:T(8,128)S(1)} all-to-all(f32[16,8,128]{2,1,0:T(8,128)S(1)} %get-tuple-element.65), channel_id=1, replica_groups=mesh['y'=8,'zh'=4,'co'=2,'zl'=2,'x'=4] {'zl','x','co'}, dimensions={0} | all-to-all | bytes 131072 | tf_op jit(solution)/shard_map/all_to_all | solution.py:24
  182.3 0.1 shard_map.119
  182.4 15.6 %all_to_all.69.x4_ref = f32[32,8,128]{2,1,0:T(8,128)S(1)} all-to-all(f32[32,8,128]{2,1,0:T(8,128)S(1)} %get-tuple-element.67), channel_id=1, replica_groups=mesh['y'=8,'zh'=4,'co'=2,'zl'=2,'x'=4] {'y','zh'}, dimensions={0} | all-to-all | bytes 262144 | tf_op jit(solution)/shard_map/all_to_all | solution.py:24
  198.0 0.9 shard_map.120
  199.0 16.8 %all_to_all.70.x5_ref = f32[16,88,128]{2,1,0:T(8,128)S(1)} all-to-all(f32[16,88,128]{2,1,0:T(8,128)S(1)} %get-tuple-element.71), channel_id=1, replica_groups=mesh['y'=8,'zh'=4,'co'=2,'zl'=2,'x'=4] {'zl','x','co'}, dimensions={0} | all-to-all | bytes 1441792 | tf_op jit(solution)/shard_map/all_to_all | solution.py:24
  215.7 1.7 shard_map.121
  (2 shorter events, 0.0 us)
Async XLA Ops:
  2.7 48.3 %copy-start = (f32[4,32,1,768]{3,2,1,0:T(1,128)S(1)}, f32[4,32,1,768]{3,2,1,0:T(1,128)}, u32[]{:S(2)}) copy-start(f32[4,32,1,768]{3,2,1,0:T(1,128)} %param.6) | copy-start | bytes 1179652
  2.7 48.3 %copy-start.1 = (f32[768,128]{1,0:T(8,128)S(1)}, f32[768,128]{1,0:T(8,128)}, u32[]{:S(2)}) copy-start(f32[768,128]{1,0:T(8,128)} %refs_3_.1) | copy-start | bytes 1179652
  2.7 48.2 %copy-start.2 = (f32[32,16]{0,1:T(8,128)S(1)}, f32[32,16]{0,1:T(8,128)}, u32[]{:S(2)}) copy-start(f32[32,16]{0,1:T(8,128)} %param.9) | copy-start | bytes 6148
  2.8 48.2 %copy-start.3 = (f32[4,8]{1,0:T(4,128)S(1)}, f32[4,8]{1,0:T(4,128)}, u32[]{:S(2)}) copy-start(f32[4,8]{1,0:T(4,128)} %e_ref.1) | copy-start | bytes 388
  2.8 48.2 %all-to-all-start = ((f32[64,2,2176]{2,1,0:T(2,128)}), f32[64,2,2176]{2,1,0:T(2,128)S(1)}, u32[]{:S(2)}, u32[]{:S(2)}) async-start(f32[64,2,2176]{2,1,0:T(2,128)} %shard_map.109), calls=%async_computation | async-start | bytes 2228224 | tf_op jit(solution)/shard_map/all_to_all | solution.py:24
